TPU v7x, 32 devices: a whole 2x2x4 slice. The times are simulated.
32 devices in a mesh: video: 2 (over y), block: 4 (over z), band: 2 (over x), chan: 2 (over core).
Axes of the slice: x: 2, y: 2, z: 4, core: 2. Of those that a mesh axis runs over, the one named last changes fastest.
Arguments:
- latents: bfloat16 [32, 2, 1664], P(('video', 'block'), 'band'), parts along dimension 0, may hold values from -60 to 60
- frame_counts: int32 [8], P('video'), parts along dimension 0, may hold values from 1 to 4, 8 in all
- w_in: bfloat16 [3, 3, 3, 16, 384], replicated, may hold values from -0.3125 to 0.3125
- gain_in: float32 [384], replicated, may hold values from 0.1 to 1.9
- shift_in: float32 [384], replicated, may hold values from -3 to 3
- w_mid: bfloat16 [3, 3, 3, 384, 384], P(None, None, None, None, 'chan'), may hold values from -0.0625 to 0.0625
- gain_out: float32 [384], P('chan'), may hold values from 0.1 to 1.9
- shift_out: float32 [384], P('chan'), may hold values from -3 to 3
Outputs:
- decoded: bfloat16 [32, 2, 104, 384], P(('video', 'block'), 'band', None, 'chan'), parts along dimension 0
There are 2 independent parts, one for each index of `video`. A program takes and returns all parts, laid end to end along the dimension named above; an argument that names none is the same for every part. Nothing has to cross between parts.
Inputs may be any that keep to these rules, and one draw needn't show every extreme that they name: `frame_counts`: entry k is the number of consecutive latent frames that device k of the frame axis holds; the entries sum to 8.
All inputs are finite; a program needn't handle non-finite values.
Results may differ from a plain program's by a relative error of at most 0.013.
Values may be sent and summed in bfloat16 or wider, within the bound.
A program may use at most 64 MiB of HBM per device.

v0:
```python
import jax
import jax.numpy as jnp
from jax import lax
from jax.sharding import PartitionSpec as P

LAT = 16
C = 384
GROUPS = 32


EPSILON = 1e-06


def with_halo(cells, sides, width):
    for axis, dim in sides:
        count = lax.axis_size(axis)
        ends = count - 1
        head = lax.slice_in_dim(cells, 0, width, axis=dim)
        tail = lax.slice_in_dim(cells, cells.shape[dim] - width, cells.shape[dim], axis=dim)
        cells = jnp.concatenate(
            [
                lax.ppermute(tail, axis, [(i, (i + 1) % count) for i in range(ends)]),
                cells,
                lax.ppermute(head, axis, [((i + 1) % count, i) for i in range(ends)]),
            ],
            axis=dim,
        )
    return cells


def count_for(frame_counts, position):
    places = jnp.arange(frame_counts.shape[0], dtype=jnp.int32)
    return jnp.sum(jnp.where(places == position, frame_counts, 0))


def start_for(frame_counts, position):
    places = jnp.arange(frame_counts.shape[0], dtype=jnp.int32)
    return jnp.sum(jnp.where(places < position, frame_counts, 0))


def rows_beside(values):
    return with_halo(values, (("band", 1),), 1)


def group_silu(values, norm_gain, norm_shift):
    in_frames, band_rows, columns, local_width = values.shape
    group_width = C // GROUPS
    local_groups = local_width // group_width
    grouped = values.reshape(in_frames, band_rows * columns, local_groups, group_width)
    group_total, squares = lax.psum(
        (jnp.sum(grouped, axis=(1, 3)), jnp.sum(grouped * grouped, axis=(1, 3))), "band"
    )
    total = float(lax.axis_size("band") * band_rows * columns * group_width)
    group_mean = group_total / total
    variance = squares / total - group_mean * group_mean
    inverse = lax.rsqrt(variance + EPSILON)
    normed = (grouped - group_mean[:, None, :, None]) * inverse[:, None, :, None]
    normed = normed.reshape(values.shape)
    return jax.nn.silu(normed * norm_gain + norm_shift)


def latent_conv(extended, kernel):
    steps_in, rows_padded, flat_width = extended.shape
    lat_width = kernel.shape[3]
    out_width = kernel.shape[4]
    columns = flat_width // lat_width
    out_frames = steps_in - 2
    band_rows = rows_padded - 2
    latent_grid = extended.reshape(steps_in, rows_padded, columns, lat_width)
    latent_grid = jnp.pad(latent_grid, ((0, 0), (0, 0), (1, 1), (0, 0)))
    patches = []
    for step_t in range(3):
        for step_y in range(3):
            for step_x in range(3):
                patches.append(
                    latent_grid[
                        step_t : step_t + out_frames,
                        step_y : step_y + band_rows,
                        step_x : step_x + columns,
                        :,
                    ]
                )
    stacked = jnp.concatenate(patches, axis=-1).reshape(-1, 27 * lat_width)
    result = jnp.dot(
        stacked, kernel.reshape(27 * lat_width, out_width), preferred_element_type=jnp.float32
    )
    return result.reshape(out_frames, band_rows, columns, out_width)


def weighted_taps(padded, kernel):
    in_frames, rows_padded, cols_padded, in_width = padded.shape
    out_frames = in_frames - 2
    band_rows = rows_padded - 2
    columns = cols_padded - 2
    out_width = kernel.shape[4]
    accumulate = jnp.zeros((out_frames * band_rows * columns, out_width), jnp.float32)
    for step_t in range(3):
        for step_y in range(3):
            patches = [
                padded[
                    step_t : step_t + out_frames,
                    step_y : step_y + band_rows,
                    step_x : step_x + columns,
                    :,
                ]
                for step_x in range(3)
            ]
            stacked = jnp.concatenate(patches, axis=-1).reshape(-1, 3 * in_width)
            accumulate = accumulate + jnp.dot(
                stacked,
                kernel[step_t, step_y].reshape(3 * in_width, out_width),
                preferred_element_type=jnp.float32,
            )
    return accumulate.reshape(out_frames, band_rows, columns, out_width)


def middle_section(act_extended, w_mid, gain_out, shift_out):
    padded = jnp.pad(rows_beside(act_extended), ((0, 0), (0, 0), (1, 1), (0, 0)))
    second_conv = weighted_taps(lax.all_gather(padded, "chan", axis=3, tiled=True), w_mid)
    second_conv = second_conv.astype(jnp.bfloat16)
    return group_silu(second_conv.astype(jnp.float32), gain_out, shift_out).astype(jnp.bfloat16)


def shards(latents, frame_counts, w_in, gain_in, shift_in, w_mid, gain_out, shift_out):
    frames, band_rows, flat_width = latents.shape
    columns = flat_width // LAT
    half_width = w_mid.shape[4]
    position = lax.axis_index("block")
    live_count = count_for(frame_counts, position)
    offset = lax.axis_index("chan") * half_width
    front_kernel = lax.dynamic_slice_in_dim(w_in, offset, half_width, 4)
    front_gain = lax.dynamic_slice_in_dim(gain_in, offset, half_width, 0)
    front_shift = lax.dynamic_slice_in_dim(shift_in, offset, half_width, 0)
    share = frames // 2
    all_slots = lax.all_gather(latents, "block", axis=0, tiled=True)
    run_ends = jnp.cumsum(frame_counts)
    run_starts = run_ends - frame_counts
    first_frame = position * share - 4
    wanted = first_frame + jnp.arange(share + 4, dtype=jnp.int32)
    owners = jnp.sum((wanted[:, None] >= run_ends[None, :]).astype(jnp.int32), axis=1)
    slot_ids = owners * frames + wanted - jnp.take(run_starts, owners)
    slot_ids = jnp.clip(slot_ids, 0, all_slots.shape[0] - 1)
    picked = jnp.take(all_slots, slot_ids, axis=0)
    latent_extended = jnp.where((wanted >= 0)[:, None, None], picked, jnp.zeros_like(picked))
    first_conv = latent_conv(rows_beside(latent_extended), front_kernel).astype(jnp.bfloat16)
    activated = group_silu(first_conv.astype(jnp.float32), front_gain, front_shift).astype(
        jnp.bfloat16
    )
    act_ids = first_frame + 2 + jnp.arange(share + 2, dtype=jnp.int32)
    act_extended = jnp.where(
        (act_ids >= 0)[:, None, None, None], activated, jnp.zeros_like(activated)
    )
    even_norm = middle_section(act_extended, w_mid, gain_out, shift_out)
    my_start = start_for(frame_counts, position)
    slot_places = jnp.arange(frames, dtype=jnp.int32)
    slot_frames = my_start + slot_places
    slot_alive = slot_places < live_count
    initial = jnp.zeros((frames, band_rows, columns, half_width), jnp.bfloat16)
    piece = lax.all_gather(even_norm, "block", axis=0, tiled=True)
    valid = (slot_frames >= 0) & (slot_frames < piece.shape[0]) & slot_alive
    took = jnp.take(piece, jnp.clip(slot_frames, 0, piece.shape[0] - 1), axis=0)
    return jnp.where(valid[:, None, None, None], took, initial)


def solution(mesh):
    return jax.shard_map(
        shards,
        mesh=mesh,
        in_specs=(
            P(("video", "block"), "band", None),
            P("video"),
            P(),
            P(),
            P(),
            P(None, None, None, None, "chan"),
            P("chan"),
            P("chan"),
        ),
        out_specs=P(("video", "block"), "band", None, "chan"),
        check_vma=False,
    )
```

profile of v0, /device:TPU:0, one launch (start us, length us, event | category | flops | bytes accessed | tf_op | source)
XLA Modules:
  0.0 121.2 jit_solution(8071006151488944462)
XLA Ops:
  0.0 0.9 reduce-window.8
  0.9 1.3 %fusion.23 = (s32[]{:T(128)}, s32[]{:T(128)}, s32[4]{0:T(128)S(1)}) fusion(s32[4]{0:T(128)} %param.9, s32[]{:T(128)S(6)} %axis_index.23, s32[4,1]{0,1:T(1,128)S(1)} %reduce-window.8), kind=kLoop, calls=%fused_computation.78 | loop fusion | flops 26 | bytes 60 | tf_op jit(solution)/shard_map/reduce_sum | solution.py:33
  3.7 15.1 %all_gather.9 = bf16[16,1,1664]{2,1,0:T(2,128)(2,1)S(1)} all-gather(bf16[4,1,1664]{2,1,0:T(2,128)(2,1)S(1)} %copy.111), channel_id=1, replica_groups=mesh['video'=2,'block'=4,'band'=2,'chan'=2] {'block'}, dimensions={0}, use_global_device_ids=true | all-gather | bytes 66560 | tf_op jit(solution)/shard_map/all_gather | solution.py:135
  19.5 1.3 %collective-permute-start.1 = (bf16[6,1,1664]{2,0,1:T(8,128)(2,1)S(1)}, bf16[6,1,1664]{2,0,1:T(8,128)(2,1)S(1)}, u32[]{:S(2)}, u32[]{:S(2)}) collective-permute-start(bf16[6,1,1664]{2,0,1:T(8,128)(2,1)S(1)} %fusion.21), channel_id=1, source_target_pairs={{2,0},{3,1},{6,4},{7,5},{10,8},{11,9},{14,12},{15,13},{18,16},{19,... | collective-permute-start | bytes 59912 | tf_op jit(solution)/shard_map/ppermute | solution.py:24
  20.8 4.5 %collective-permute-start = (bf16[6,1,1664]{2,0,1:T(8,128)(2,1)S(1)}, bf16[6,1,1664]{2,0,1:T(8,128)(2,1)S(1)}, u32[]{:S(2)}, u32[]{:S(2)}) collective-permute-start(bf16[6,1,1664]{2,0,1:T(8,128)(2,1)S(1)} %fusion.21), channel_id=1, source_target_pairs={{0,2},{1,3},{4,6},{5,7},{8,10},{9,11},{12,14},{13,15},{16,18},{17,... | collective-permute-start | bytes 59912 | tf_op jit(solution)/shard_map/ppermute | solution.py:22
  26.4 3.6 %fusion.32 = (bf16[1,1,3,384,192]{3,4,2,1,0:T(8,128)(2,1)S(1)}, bf16[1,1,3,384,192]{3,4,2,1,0:T(8,128)(2,1)S(1)}, bf16[1,1,3,384,192]{3,4,2,1,0:T(8,128)(2,1)S(1...) fusion(bf16[3,3,3,384,192]{3,4,2,1,0:T(8,128)(2,1)} %param.13), kind=kLoop, calls=%fused_computation.95 | loop fusion | bytes 7962624 | tf_op jit(solution)/shard_map/slice | solution.py:111
  30.7 1.8 %compare_and_fusion.1 = (pred[4]{0:T(512)(128)(4,1)}, pred[4]{0:T(512)(128)(4,1)}) fusion(s32[]{:T(128)} %get-tuple-element.10, s32[]{:T(128)} %get-tuple-element.9), kind=kLoop, calls=%fused_computation.71 | loop fusion | flops 52 | bytes 16 | tf_op jit(solution)/shard_map/jit(_take)/and | solution.py:161
  35.1 1.3 %fusion.35 = (bf16[4,1,104,16]{3,2,0,1:T(8,128)(2,1)}, bf16[4,1,104,16]{3,2,0,1:T(8,128)(2,1)}, bf16[4,1,104,16]{3,2,0,1:T(8,128)(2,1)}, bf16[4,1,104,16]{3,2,0,...) fusion(bf16[6,3,106,16]{3,2,0,1:T(8,128)(2,1)S(1)} %fusion.14), kind=kLoop, calls=%fused_computation.98 | loop fusion | bytes 479232 | tf_op jit(solution)/shard_map/slice | solution.py:76
  38.8 1.5 %slice.245 = bf16[4,1,104,16]{3,2,0,1:T(8,128)(2,1)} reshape(bf16[4,1,1664]{2,0,1:T(4,128)(2,1)} %get-tuple-element.73) | data formatting | bytes 26624 | tf_op jit(solution)/shard_map/slice | solution.py:76
  41.0 1.5 %slice.256 = bf16[4,1,104,16]{3,2,0,1:T(8,128)(2,1)} reshape(bf16[4,1,1664]{2,0,1:T(4,128)(2,1)} %get-tuple-element.72) | data formatting | bytes 26624 | tf_op jit(solution)/shard_map/slice | solution.py:76
  42.5 4.0 %concatenate.44 = bf16[4,1,104,432]{3,2,0,1:T(8,128)(2,1)} concatenate(bf16[4,1,104,16]{3,2,0,1:T(8,128)(2,1)} %get-tuple-element.68, bf16[4,1,104,16]{3,2,0,1:T(8,128)(2,1)S(1)} %slice.227, bf16[4,1,104,16]{3,2,0,1:T(8,128)(2,1)} %get-tuple-element.67, bf16[4,1,104,16]{3,2,0,1:T(8,128)(2,1)} %get-tuple-element.66, bf16[4,1,104,16]{3,2,0,1:T(8,128)(2,1)S(1)} %copy-done.18, ...), dimensions={3} | concatenate | bytes 718848 | tf_op jit(solution)/shard_map/concatenate | solution.py:83
  46.5 2.2 %fusion.30 = (f32[4,192]{1,0:T(4,128)S(1)}, f32[4,192]{1,0:T(4,128)S(1)}, f32[4,104,192]{1,2,0:T(8,128)}) fusion(bf16[432,192,1]{1,0,2:T(8,128)(2,1)} %bitcast.174, bf16[4,1,104,432]{3,2,0,1:T(8,128)(2,1)} %concatenate.44), kind=kOutput, calls=%fused_computation.93 | convolution fusion | flops 69407232 | bytes 850944 | tf_op jit(solution)/shard_map/dot_general | solution.py:84
  49.1 4.9 %all-reduce.3 = (f32[4,16]{1,0:T(4,128)S(1)}, f32[4,16]{1,0:T(4,128)S(1)}) all-reduce(f32[4,16]{1,0:T(4,128)S(1)} %reduce_sum.88, f32[4,16]{1,0:T(4,128)S(1)} %reduce_sum.85), channel_id=1, replica_groups=mesh['video'=2,'block'=4,'band'=2,'chan'=2] {'band'}, use_global_device_ids=true, to_apply=%region_9.10 | all-reduce | flops 128 | bytes 1024 | tf_op jit(solution)/shard_map/psum | solution.py:50
  54.4 1.3 %select_bitcast_fusion = bf16[4,1,104,192]{2,3,0,1:T(8,128)(2,1)S(1)} fusion(f32[192]{0:T(256)S(1)} %copy-done.19, f32[192]{0:T(256)S(1)} %copy-done.20, f32[4,192]{1,0:T(4,128)S(1)} %mul.122, f32[4,104,192]{1,2,0:T(8,128)} %get-tuple-element.83, f32[4,192]{1,0:T(4,128)S(1)} %sub.66, pred[4]{0:T(512)(128)(4,1)S(1)} %copy-done.27), kind=kLoop, calls=%fused_computation.52 | loop fusion | flops 798720 | bytes 486916 | tf_op jit(solution)/shard_map/jit(_where)/select_n | solution.py:150
  55.8 1.3 %collective-permute-start.3 = (bf16[4,1,104,192]{2,3,0,1:T(8,128)(2,1)S(1)}, bf16[4,1,104,192]{2,3,0,1:T(8,128)(2,1)S(1)}, u32[]{:S(2)}, u32[]{:S(2)}) collective-permute-start(bf16[4,1,104,192]{2,3,0,1:T(8,128)(2,1)S(1)} %select_bitcast_fusion), channel_id=1, source_target_pairs={{2,0},{3,1},{6,4},{7,5},{10,8},{11,9},{14,12},{15,13},{18,16},{19,... | collective-permute-start | bytes 479240 | tf_op jit(solution)/shard_map/ppermute | solution.py:24
  57.1 4.6 %collective-permute-start.2 = (bf16[4,1,104,192]{2,3,0,1:T(8,128)(2,1)S(1)}, bf16[4,1,104,192]{2,3,0,1:T(8,128)(2,1)S(1)}, u32[]{:S(2)}, u32[]{:S(2)}) collective-permute-start(bf16[4,1,104,192]{2,3,0,1:T(8,128)(2,1)S(1)} %select_bitcast_fusion), channel_id=1, source_target_pairs={{0,2},{1,3},{4,6},{5,7},{8,10},{9,11},{12,14},{13,15},{16,18},{17,... | collective-permute-start | bytes 479240 | tf_op jit(solution)/shard_map/ppermute | solution.py:22
  70.6 0.8 copy.144
  74.2 2.8 %all_gather.10 = bf16[4,3,106,384]{2,3,0,1:T(8,128)(2,1)S(1)} all-gather(bf16[4,3,106,192]{2,3,0,1:T(8,128)(2,1)S(1)} %fusion.12), channel_id=1, replica_groups=mesh['video'=2,'block'=4,'band'=2,'chan'=2] {'chan'}, dimensions={3}, use_global_device_ids=true | all-gather | bytes 1465344 | tf_op jit(solution)/shard_map/all_gather | solution.py:119
  77.4 2.3 %fusion.33 = (bf16[2,1,104,384]{2,3,0,1:T(8,128)(2,1)S(1)}, bf16[2,1,104,384]{2,3,0,1:T(8,128)(2,1)}, bf16[2,1,104,384]{2,3,0,1:T(8,128)(2,1)}, bf16[2,1,104,384...) fusion(bf16[4,3,106,384]{2,3,0,1:T(8,128)(2,1)S(1)} %all_gather.10), kind=kLoop, calls=%fused_computation.96 | loop fusion | bytes 6070272 | tf_op jit(solution)/shard_map/slice | solution.py:100
  79.8 1.0 copy.113
  82.3 1.1 pad_maximum_fusion.3
  83.7 1.0 pad_maximum_fusion.4
  85.0 1.2 %pad_maximum_fusion.5 = bf16[2,1,104,1152]{2,3,0,1:T(8,128)(2,1)S(1)} fusion(bf16[2,1,104,384]{2,3,0,1:T(8,128)(2,1)} %get-tuple-element.33, bf16[2,1,104,384]{2,3,0,1:T(8,128)(2,1)} %get-tuple-element.34, bf16[2,1,104,384]{2,3,0,1:T(8,128)(2,1)} %get-tuple-element.35), kind=kLoop, calls=%fused_computation.34 | loop fusion | flops 1437696 | bytes 958464 | tf_op jit(solution)/shard_map/concatenate | solution.py:108
  86.6 1.2 %pad_maximum_fusion.6 = bf16[2,1,104,1152]{2,3,0,1:T(8,128)(2,1)S(1)} fusion(bf16[2,1,104,384]{2,3,0,1:T(8,128)(2,1)} %get-tuple-element.30, bf16[2,1,104,384]{2,3,0,1:T(8,128)(2,1)} %get-tuple-element.31, bf16[2,1,104,384]{2,3,0,1:T(8,128)(2,1)} %get-tuple-element.32), kind=kLoop, calls=%fused_computation.35 | loop fusion | flops 1437696 | bytes 958464 | tf_op jit(solution)/shard_map/concatenate | solution.py:108
  87.8 1.1 copy.125
  88.9 1.2 %pad_maximum_fusion.7 = bf16[2,1,104,1152]{2,3,0,1:T(8,128)(2,1)S(1)} fusion(bf16[2,1,104,384]{2,3,0,1:T(8,128)(2,1)} %get-tuple-element.27, bf16[2,1,104,384]{2,3,0,1:T(8,128)(2,1)} %get-tuple-element.28, bf16[2,1,104,384]{2,3,0,1:T(8,128)(2,1)} %get-tuple-element.29), kind=kLoop, calls=%fused_computation.36 | loop fusion | flops 1437696 | bytes 958464 | tf_op jit(solution)/shard_map/concatenate | solution.py:108
  90.1 1.0 copy.127
  91.2 1.1 pad_maximum_fusion.8
  92.3 1.0 copy.129
  93.4 1.6 %fusion.39 = f32[208,192]{0,1:T(8,128)S(1)} fusion(bf16[208,1152]{1,0:T(8,128)(2,1)} %bitcast.162, bf16[1152,192]{0,1:T(8,128)(2,1)} %bitcast.163), kind=kOutput, calls=%fused_computation.102 | convolution fusion | flops 92012544 | bytes 1081344 | tf_op jit(solution)/shard_map/dot_general | solution.py:109
  99.9 4.9 %all-reduce.2 = (f32[2,16]{1,0:T(2,128)S(1)}, f32[2,16]{1,0:T(2,128)S(1)}) all-reduce(f32[2,16]{1,0:T(2,128)S(1)} %copy.133, f32[2,16]{1,0:T(2,128)S(1)} %copy.131), channel_id=1, replica_groups=mesh['video'=2,'block'=4,'band'=2,'chan'=2] {'band'}, use_global_device_ids=true, to_apply=%region_13.14 | all-reduce | flops 64 | bytes 512 | tf_op jit(solution)/shard_map/psum | solution.py:50
  105.4 14.3 %all_gather.11 = bf16[8,1,104,192]{2,3,1,0:T(8,128)(2,1)S(1)} all-gather(bf16[2,1,104,192]{2,3,1,0:T(8,128)(2,1)S(1)} %multiply_convert_fusion.1), channel_id=1, replica_groups=mesh['video'=2,'block'=4,'band'=2,'chan'=2] {'block'}, dimensions={0}, use_global_device_ids=true | all-gather | bytes 399360 | tf_op jit(solution)/shard_map/all_gather | solution.py:159
  (147 shorter events, 31.5 us)
Async XLA Ops:
  0.0 29.9 %copy-start = (bf16[3,3,3,16,384]{4,3,2,1,0:T(8,128)(2,1)S(1)}, bf16[3,3,3,16,384]{4,3,2,1,0:T(8,128)(2,1)}, u32[]{:S(2)}) copy-start(bf16[3,3,3,16,384]{4,3,2,1,0:T(8,128)(2,1)} %param.10) | copy-start | bytes 995332
  19.5 15.0 %collective-permute-start.1 = (bf16[6,1,1664]{2,0,1:T(8,128)(2,1)S(1)}, bf16[6,1,1664]{2,0,1:T(8,128)(2,1)S(1)}, u32[]{:S(2)}, u32[]{:S(2)}) collective-permute-start(bf16[6,1,1664]{2,0,1:T(8,128)(2,1)S(1)} %fusion.21), channel_id=1, source_target_pairs={{2,0},{3,1},{6,4},{7,5},{10,8},{11,9},{14,12},{15,13},{18,16},{19,... | collective-permute-start | bytes 59912 | tf_op jit(solution)/shard_map/ppermute | solution.py:24
  20.8 13.9 %collective-permute-start = (bf16[6,1,1664]{2,0,1:T(8,128)(2,1)S(1)}, bf16[6,1,1664]{2,0,1:T(8,128)(2,1)S(1)}, u32[]{:S(2)}, u32[]{:S(2)}) collective-permute-start(bf16[6,1,1664]{2,0,1:T(8,128)(2,1)S(1)} %fusion.21), channel_id=1, source_target_pairs={{0,2},{1,3},{4,6},{5,7},{8,10},{9,11},{12,14},{13,15},{16,18},{17,... | collective-permute-start | bytes 59912 | tf_op jit(solution)/shard_map/ppermute | solution.py:22
  26.4 6.8 %copy-start.25 = (f32[384]{0:T(512)S(1)}, f32[384]{0:T(512)}, u32[]{:S(2)}) copy-start(f32[384]{0:T(512)} %param.12) | copy-start | bytes 4612
  26.4 7.5 %copy-start.26 = (f32[384]{0:T(512)S(1)}, f32[384]{0:T(512)}, u32[]{:S(2)}) copy-start(f32[384]{0:T(512)} %param.11) | copy-start | bytes 4612
  35.0 7.5 %copy-start.16 = (bf16[4,1,104,16]{3,2,0,1:T(8,128)(2,1)S(1)}, bf16[4,1,104,16]{3,2,0,1:T(8,128)(2,1)}, u32[]{:S(2)}) copy-start(bf16[4,1,104,16]{3,2,0,1:T(8,128)(2,1)} %get-tuple-element.69) | copy-start | bytes 39940
  35.0 7.5 %copy-start.17 = (bf16[4,1,104,16]{3,2,0,1:T(8,128)(2,1)S(1)}, bf16[4,1,104,16]{3,2,0,1:T(8,128)(2,1)}, u32[]{:S(2)}) copy-start(bf16[4,1,104,16]{3,2,0,1:T(8,128)(2,1)} %get-tuple-element.70) | copy-start | bytes 39940
  35.1 7.5 %copy-start.18 = (bf16[4,1,104,16]{3,2,0,1:T(8,128)(2,1)S(1)}, bf16[4,1,104,16]{3,2,0,1:T(8,128)(2,1)}, u32[]{:S(2)}) copy-start(bf16[4,1,104,16]{3,2,0,1:T(8,128)(2,1)} %get-tuple-element.71) | copy-start | bytes 39940
  46.5 7.9 %copy-start.19 = (f32[192]{0:T(256)S(1)}, f32[192]{0:T(256)}, u32[]{:S(2)}) copy-start(f32[192]{0:T(256)} %dynamic_slice.11) | copy-start | bytes 2308
  46.5 7.9 %copy-start.20 = (f32[192]{0:T(256)S(1)}, f32[192]{0:T(256)}, u32[]{:S(2)}) copy-start(f32[192]{0:T(256)} %dynamic_slice.10) | copy-start | bytes 2308
  46.5 7.9 %copy-start.27 = (pred[4]{0:T(512)(128)(4,1)S(1)}, pred[4]{0:T(512)(128)(4,1)}, u32[]{:S(2)}) copy-start(pred[4]{0:T(512)(128)(4,1)} %add_compare_fusion) | copy-start | bytes 16
  46.5 15.8 %copy-start.14 = (bf16[1,1,3,384,192]{3,4,2,1,0:T(8,128)(2,1)S(1)}, bf16[1,1,3,384,192]{3,4,2,1,0:T(8,128)(2,1)}, u32[]{:S(2)}) copy-start(bf16[1,1,3,384,192]{3,4,2,1,0:T(8,128)(2,1)} %get-tuple-element.22) | copy-start | bytes 1327108
  55.8 18.1 %collective-permute-start.3 = (bf16[4,1,104,192]{2,3,0,1:T(8,128)(2,1)S(1)}, bf16[4,1,104,192]{2,3,0,1:T(8,128)(2,1)S(1)}, u32[]{:S(2)}, u32[]{:S(2)}) collective-permute-start(bf16[4,1,104,192]{2,3,0,1:T(8,128)(2,1)S(1)} %select_bitcast_fusion), channel_id=1, source_target_pairs={{2,0},{3,1},{6,4},{7,5},{10,8},{11,9},{14,12},{15,13},{18,16},{19,... | collective-permute-start | bytes 479240 | tf_op jit(solution)/shard_map/ppermute | solution.py:24
  57.1 16.8 %collective-permute-start.2 = (bf16[4,1,104,192]{2,3,0,1:T(8,128)(2,1)S(1)}, bf16[4,1,104,192]{2,3,0,1:T(8,128)(2,1)S(1)}, u32[]{:S(2)}, u32[]{:S(2)}) collective-permute-start(bf16[4,1,104,192]{2,3,0,1:T(8,128)(2,1)S(1)} %select_bitcast_fusion), channel_id=1, source_target_pairs={{0,2},{1,3},{4,6},{5,7},{8,10},{9,11},{12,14},{13,15},{16,18},{17,... | collective-permute-start | bytes 479240 | tf_op jit(solution)/shard_map/ppermute | solution.py:22
  62.7 1.1 copy-start.13
  64.2 1.1 copy-start.12
  80.9 0.9 copy-start.15
  93.4 1.6 %copy-start.4 = (bf16[24,8,3,384]{3,1,2,0:T(8,128)(2,1)S(1)}, bf16[24,8,3,384]{3,1,2,0:T(8,128)(2,1)}, u32[]{:S(2)}) copy-start(bf16[24,8,3,384]{3,1,2,0:T(8,128)(2,1)} %copy.139) | copy-start | bytes 1327108
  93.4 1.9 %copy-start.5 = (bf16[24,8,3,384]{3,1,2,0:T(8,128)(2,1)S(1)}, bf16[24,8,3,384]{3,1,2,0:T(8,128)(2,1)}, u32[]{:S(2)}) copy-start(bf16[24,8,3,384]{3,1,2,0:T(8,128)(2,1)} %copy.140) | copy-start | bytes 1327108
  94.9 1.0 copy-start.6
  95.3 1.0 copy-start.7
  95.9 1.0 copy-start.8
  96.3 1.1 copy-start.1
  96.3 1.2 copy-start.9
  97.0 1.1 copy-start.2
  97.0 1.2 %copy-start.10 = (bf16[24,8,3,384]{3,1,2,0:T(8,128)(2,1)S(1)}, bf16[24,8,3,384]{3,1,2,0:T(8,128)(2,1)}, u32[]{:S(2)}) copy-start(bf16[24,8,3,384]{3,1,2,0:T(8,128)(2,1)} %copy.145) | copy-start | bytes 1327108
  97.5 1.1 copy-start.3
  97.5 1.2 %copy-start.11 = (bf16[24,8,3,384]{3,1,2,0:T(8,128)(2,1)S(1)}, bf16[24,8,3,384]{3,1,2,0:T(8,128)(2,1)}, u32[]{:S(2)}) copy-start(bf16[24,8,3,384]{3,1,2,0:T(8,128)(2,1)} %copy.146) | copy-start | bytes 1327108
  98.7 6.4 %copy-start.23 = (f32[192]{0:T(256)S(1)}, f32[192]{0:T(256)}, u32[]{:S(2)}) copy-start(f32[192]{0:T(256)} %param.15) | copy-start | bytes 2308
  98.7 6.4 %copy-start.24 = (f32[192]{0:T(256)S(1)}, f32[192]{0:T(256)}, u32[]{:S(2)}) copy-start(f32[192]{0:T(256)} %param.14) | copy-start | bytes 2308
  99.1 21.3 %copy-start.21 = (pred[4]{0:T(512)(128)(4,1)S(1)}, pred[4]{0:T(512)(128)(4,1)}, u32[]{:S(2)}) copy-start(pred[4]{0:T(512)(128)(4,1)} %get-tuple-element.84) | copy-start | bytes 16
  99.1 21.3 %copy-start.22 = (pred[4]{0:T(512)(128)(4,1)S(1)}, pred[4]{0:T(512)(128)(4,1)}, u32[]{:S(2)}) copy-start(pred[4]{0:T(512)(128)(4,1)} %get-tuple-element.85) | copy-start | bytes 16
where the time goes:
time: 122 us; the launch traced here: 121 us
  local copies, waits for them, and re-layouts  44.2 us (36%)
  blocking collectives  42.1 us (35%)
  other arithmetic  16.3 us (13%)
  starting transfers between devices  11.7 us (10%)
  matrix products  6.32 us (5%)
    all_gather x1, blocking collectives, shards(): all_slots = lax.all_gather(latents, 'block', axis=0, tiled=True)  15.1 us
    all_gather x1, blocking collectives, shards(): piece = lax.all_gather(even_norm, 'block', axis=0, tiled=True)  14.3 us
    unnamed x67, local copies, waits for them, and re-layouts  11 us
    psum x2, blocking collectives, group_silu(): lax.psum((jnp.sum(grouped, axis=(1, 3)), jnp.sum(grouped * grouped, axis=...  9.85 us
    ppermute x2, starting transfers between devices, with_halo(): lax.ppermute(tail, axis, [(i, (i + 1) % count) for i in range(ends)])  9.11 us
    slice x10, local copies, waits for them, and re-layouts, latent_conv(): latent_grid[step_t:step_t + out_frames, step_y:step_y + band_rows, step_x...  8.19 us
    concatenate x9, other arithmetic, weighted_taps(): stacked = jnp.concatenate(patches, axis=-1).reshape(-1, 3 * in_width)  7.39 us
    slice x10, local copies, waits for them, and re-layouts, weighted_taps(): kernel[step_t, step_y].reshape(3 * in_width, out_width)  6.99 us
  transfers between devices with their start and end apart: 4, of which 0 were waited for; matrix products, arithmetic and copies ran while one was open for 17% of the time, Pallas kernels for 0%

commit v1 on v0

v1 whole, which is shorter than its diff:
```python
import functools

import jax
import jax.numpy as jnp
from jax import lax
from jax.experimental import pallas as pl
from jax.experimental.pallas import tpu as pltpu
from jax.sharding import PartitionSpec as P

LAT = 16
C = 384
GROUPS = 32
GW = C // GROUPS
EPSILON = 1e-06
MESH = pl.DeviceIdType.MESH
F32 = jnp.float32
BF16 = jnp.bfloat16


def up(n, m):
    return (n + m - 1) // m * m


def rows_for(r, R):
    return tuple(range(max(0, r - 1), min(R - 1, r + 1) + 1))


def group_matrix(n):
    a = lax.broadcasted_iota(jnp.int32, (n, n), 0)
    b = lax.broadcasted_iota(jnp.int32, (n, n), 1)
    same = ((a * 5462) >> 16) == ((b * 5462) >> 16)
    return jnp.where(same, 1.0, 0.0).astype(BF16)


def group_sums(x, gmat):
    hi = x.astype(BF16)
    rest = x - hi.astype(F32)
    mid = rest.astype(BF16)
    lo = (rest - mid.astype(F32)).astype(BF16)
    n = x.shape[0]
    y = jnp.dot(
        jnp.concatenate([hi, mid, lo], axis=0), gmat, preferred_element_type=F32
    )
    return y[:n] + y[n : 2 * n] + y[2 * n :]


def silu(u):
    return u / (1.0 + jnp.exp(-u))


def body(
    nb, R, COLS, SL, reach,
    cnt_ref, lat_ref, win_ref, gin_ref, sin_ref, wmid_ref, gout_ref, sout_ref,
    out_ref,
    slots, xf, gf, wpad, c1s, la, lb, wv, stats,
    send_sem, recv_sem, st_send, st_recv, w_sem, win_sem,
):
    k = lax.axis_index("block")
    b = lax.axis_index("band")
    half = out_ref.shape[1]
    FL = SL + 4
    FA = SL + 2
    nin = min(3, R)
    sets = sorted(set(rows_for(r, R) for r in range(R)))

    y0 = 1 - b if R == 2 else 0
    wcopies = []
    for t in range(3):
        c = pltpu.make_async_copy(
            wmid_ref.at[t, pl.ds(y0, nin)], wv.at[t], w_sem.at[t]
        )
        wcopies.append(c)
    wincopies = []
    kpad = wpad.shape[1] // 3
    for r in range(R):
        rows = rows_for(r, R)
        first = (rows[0] - r + 1) * 3 * LAT
        size = len(rows) * 3 * LAT
        for t in range(3):
            c = pltpu.make_async_copy(
                win_ref.at[t, pl.ds(first, size)],
                wpad.at[r, pl.ds(t * kpad, size)],
                win_sem.at[r, t],
            )
            wincopies.append(c)
    barrier = pltpu.get_barrier_semaphore()
    pairs = [(d, o) for d in range(reach + 1) for o in range(R) if (d, o) != (0, 0)]
    for d, o in pairs:
        @pl.when(k >= d)
        def _():
            pl.semaphore_signal(
                barrier, inc=1,
                device_id={"block": k - d, "band": lax.rem(b + R - o, R)},
                device_id_type=MESH,
            )
    for c in wincopies:
        c.start()
    for c in wcopies:
        c.start()
    own = lat_ref[...]
    slots[0, b] = own
    for r in range(R):
        size = len(rows_for(r, R)) * 3 * LAT
        if size < kpad:
            for t in range(3):
                wpad[r, t * kpad + size : (t + 1) * kpad, :] = jnp.zeros((kpad - size, C), BF16)
    pl.semaphore_wait(barrier, jnp.minimum(reach + 1, nb - k) * R - 1)

    def copy_to(d, o):
        return pltpu.make_async_remote_copy(
            src_ref=lat_ref,
            dst_ref=slots.at[d, b],
            send_sem=send_sem.at[d, o],
            recv_sem=recv_sem.at[d, o],
            device_id={"block": k + d, "band": lax.rem(b + o, R)},
            device_id_type=MESH,
        )

    def copy_from(d, o):
        return pltpu.make_async_remote_copy(
            src_ref=lat_ref,
            dst_ref=slots.at[d, lax.rem(b + R - o, R)],
            send_sem=send_sem.at[d, o],
            recv_sem=recv_sem.at[d, o],
            device_id={"block": k, "band": lax.rem(b + o, R)},
            device_id_type=MESH,
        )

    for d, o in reversed(pairs):
        @pl.when(k + d < nb)
        def _():
            copy_to(d, o).start()

    sel = {}
    for rows in sets:
        n = len(rows)
        a = lax.broadcasted_iota(jnp.int32, (n * 3 * 128, kpad), 0)
        c = lax.broadcasted_iota(jnp.int32, (n * 3 * 128, kpad), 1)
        hit = ((a >> 7) * LAT + (a & (LAT - 1))) == c
        sel[rows] = jnp.where(hit, 1.0, 0.0).astype(BF16)
    gmat = group_matrix(C)

    e = [jnp.int32(0)]
    for d in range(1, reach + 1):
        n = cnt_ref[jnp.maximum(k - d, 0)]
        e.append(e[-1] + jnp.where(k >= d, n, 0))
    before = e[-1]

    for d, o in pairs:
        @pl.when(k >= d)
        def _():
            copy_from(d, o).wait_recv()

    for d in range(reach + 1):
        for r in range(R):
            xf[d * R + r] = slots[d, r].astype(F32)

    W = COLS * LAT
    lane = lax.broadcasted_iota(jnp.int32, (8, W), 1)
    sub = lax.broadcasted_iota(jnp.int32, (8, W), 0)
    part = (lane >> 4) & 7
    mask = [part == ((sub + 7) & 7), part == sub, part == ((sub + 1) & 7)]
    zero128 = jnp.zeros((8, 128), F32)

    def expanded(j, r):
        if j >= 4:
            row = xf[r, j - 4 : j - 3, :]
        else:
            m = 4 - j
            d = jnp.int32(1)
            base = e[1]
            for q in range(1, reach):
                more = e[q] < m
                d = jnp.where(more, q + 1, d)
                base = jnp.where(more, e[q + 1], base)
            slot = jnp.clip(base - m, 0, SL - 1)
            row = xf[d * R + r, pl.ds(slot, 1), :]
            row = jnp.where(jnp.broadcast_to(before >= m, row.shape), row, 0.0)
        bc = jnp.broadcast_to(row, (8, W))
        prev = jnp.concatenate([zero128, bc[:, : W - 128]], axis=1)
        nxt = jnp.concatenate([bc[:, 128:], zero128], axis=1)
        ys = [
            jnp.where(mask[0], jnp.where(sub == 0, prev, bc), 0.0),
            jnp.where(mask[1], bc, 0.0),
            jnp.where(mask[2], jnp.where(sub == 7, nxt, bc), 0.0),
        ]
        return [
            jnp.concatenate([y[:, q * 128 : q * 128 + 128] for q in range(W // 128)], axis=0)
            for y in ys
        ]

    for p in range(FL // 2):
        ex = {}
        for r in range(R):
            u, v = expanded(2 * p, r), expanded(2 * p + 1, r)
            ex[r] = [jnp.concatenate([u[x], v[x]], axis=0).astype(BF16) for x in range(3)]
        for i, rows in enumerate(sets):
            lhs = jnp.concatenate([ex[r][x] for r in rows for x in range(3)], axis=1)
            gf[i, p * 2 * COLS : (p + 1) * 2 * COLS, :] = jnp.dot(
                lhs, sel[rows], preferred_element_type=F32
            )

    for c in wincopies:
        c.wait()
    MA = FA * COLS
    for r in range(R):
        i = sets.index(rows_for(r, R))
        lhs = jnp.concatenate(
            [gf[i, t * COLS : t * COLS + MA, :] for t in range(3)], axis=1
        ).astype(BF16)
        c1s[r] = jnp.dot(lhs, wpad[r], preferred_element_type=F32).astype(BF16).astype(F32)

    s1, s2 = [], []
    for f in range(FA):
        a1 = a2 = None
        for r in range(R):
            h = c1s[r, f * COLS : (f + 1) * COLS, :]
            p1 = jnp.sum(h, axis=0, keepdims=True)
            p2 = jnp.sum(h * h, axis=0, keepdims=True)
            a1 = p1 if a1 is None else a1 + p1
            a2 = p2 if a2 is None else a2 + p2
        s1.append(a1)
        s2.append(a2)
    fill = jnp.zeros((16 - 2 * FA, C), F32)
    g = group_sums(jnp.concatenate(s1 + s2 + [fill], axis=0), gmat)
    total = float(R * COLS * GW)
    mean = g[:FA] / total
    var = g[FA : 2 * FA] / total - mean * mean
    inv = lax.rsqrt(var + EPSILON)
    scale = inv * gin_ref[...]
    shift = sin_ref[...] - mean * scale

    off = 0 if R == 2 else 1
    if off:
        for z in (0, R + 1):
            la[z] = jnp.zeros(la.shape[1:], BF16)
            lb[z] = jnp.zeros(lb.shape[1:], BF16)
    for r in range(R):
        act = []
        for f in range(FA):
            u = c1s[r, f * COLS : (f + 1) * COLS, :] * scale[f : f + 1] + shift[f : f + 1]
            a = silu(u)
            if f < 2:
                a = jnp.where(jnp.broadcast_to(before >= 2 - f, a.shape), a, 0.0)
            act.append(a)
        for p in range(FA // 2):
            la[r + off, p * 2 * COLS : (p + 1) * 2 * COLS, :] = jnp.concatenate(
                act[2 * p : 2 * p + 2], axis=0
            ).astype(BF16)
        for p in range(SL // 2):
            lb[r + off, p * 2 * COLS : (p + 1) * 2 * COLS, :] = jnp.concatenate(
                act[2 * p + 1 : 2 * p + 3], axis=0
            ).astype(BF16)

    for c in wcopies:
        c.wait()
    M = SL * COLS
    first = 0 if R == 2 else b
    lhs = []
    for t in range(3):
        for q in range(nin):
            if t == 1:
                lhs.append(lb[first + q])
            else:
                lhs.append(la[first + q, t * COLS : t * COLS + M, :])
    lhs = jnp.concatenate(lhs, axis=1)
    prod = []
    for x in range(3):
        rhs = jnp.concatenate([wv[t, q, x] for t in range(3) for q in range(nin)], axis=1)
        prod.append(
            lax.dot_general(
                lhs, rhs, (((1,), (1,)), ((), ())), preferred_element_type=F32
            )
        )
    hs, t1, t2 = [], [], []
    col = lax.broadcasted_iota(jnp.int32, (COLS, half), 0)
    for f in range(SL):
        p0, p1, p2 = [p[f * COLS : (f + 1) * COLS] for p in prod]
        h = p1 + jnp.where(col == 0, 0.0, pltpu.roll(p0, 1, 0))
        h = h + jnp.where(col == COLS - 1, 0.0, pltpu.roll(p2, COLS - 1, 0))
        h = h.astype(BF16).astype(F32)
        hs.append(h)
        t1.append(jnp.sum(h, axis=0, keepdims=True))
        t2.append(jnp.sum(h * h, axis=0, keepdims=True))
    stats[b] = jnp.concatenate(t1 + t2, axis=0)

    def stat_copy(o, place):
        return pltpu.make_async_remote_copy(
            src_ref=stats.at[place],
            dst_ref=stats.at[place],
            send_sem=st_send.at[o],
            recv_sem=st_recv.at[o],
            device_id={"band": lax.rem(b + o, R)},
            device_id_type=MESH,
        )

    for o in range(1, R):
        stat_copy(o, b).start()
    gmat2 = group_matrix(half)
    for o in range(1, R):
        stat_copy(o, lax.rem(b + R - o, R)).wait_recv()
    both = stats[0]
    for r in range(1, R):
        both = both + stats[r]
    pad = jnp.zeros((16 - 2 * SL, half), F32)
    g = group_sums(jnp.concatenate([both, pad], axis=0), gmat2)
    mean = g[:SL] / total
    var = g[SL : 2 * SL] / total - mean * mean
    inv = lax.rsqrt(var + EPSILON)
    scale = inv * gout_ref[...]
    shift = sout_ref[...] - mean * scale
    for f in range(SL):
        a = silu(hs[f] * scale[f : f + 1] + shift[f : f + 1])
        out_ref[f] = a.T.astype(BF16)

    for d, o in pairs:
        @pl.when(k + d < nb)
        def _():
            copy_to(d, o).wait_send()
    for o in range(1, R):
        stat_copy(o, b).wait_send()


def shards(latents, frame_counts, w_in, gain_in, shift_in, w_mid, gain_out, shift_out):
    SL, band_rows, width = latents.shape
    COLS = width // LAT
    half = w_mid.shape[4]
    R = lax.axis_size("band") * band_rows
    nb = lax.axis_size("block")
    reach = min(4, nb - 1)
    nin = min(3, R)
    FL, FA = SL + 4, SL + 2
    sets = set(rows_for(r, R) for r in range(R))
    kpad = up(max(len(s) for s in sets) * 3 * LAT, 128)
    extra = 0 if R == 2 else 2
    vmem = pl.BlockSpec(memory_space=pltpu.VMEM)
    hbm = pl.BlockSpec(memory_space=pl.ANY)
    raw = pl.pallas_call(
        functools.partial(body, nb, R, COLS, SL, reach),
        out_shape=jax.ShapeDtypeStruct((SL, half, COLS), BF16),
        in_specs=[
            pl.BlockSpec(memory_space=pltpu.SMEM), vmem, hbm, vmem, vmem, hbm, vmem, vmem,
        ],
        out_specs=vmem,
        scratch_shapes=[
            pltpu.VMEM((reach + 1, R, SL, width), BF16),
            pltpu.VMEM(((reach + 1) * R, SL, width), F32),
            pltpu.VMEM((len(sets), FL * COLS, kpad), F32),
            pltpu.VMEM((R, 3 * kpad, C), BF16),
            pltpu.VMEM((R, FA * COLS, C), F32),
            pltpu.VMEM((R + extra, FA * COLS, C), BF16),
            pltpu.VMEM((R + extra, SL * COLS, C), BF16),
            pltpu.VMEM((3, nin, 3, half, C), BF16),
            pltpu.VMEM((R, 2 * SL, half), F32),
            pltpu.SemaphoreType.DMA((reach + 1, R)),
            pltpu.SemaphoreType.DMA((reach + 1, R)),
            pltpu.SemaphoreType.DMA((R,)),
            pltpu.SemaphoreType.DMA((R,)),
            pltpu.SemaphoreType.DMA((3,)),
            pltpu.SemaphoreType.DMA((R, 3)),
        ],
        compiler_params=pltpu.CompilerParams(
            collective_id=0, has_side_effects=True, vmem_limit_bytes=56 * 1024 * 1024
        ),
    )(
        frame_counts,
        latents.reshape(SL, width),
        w_in.reshape(3, 9 * LAT, C),
        gain_in.reshape(1, C),
        shift_in.reshape(1, C),
        jnp.swapaxes(w_mid, 3, 4),
        gain_out.reshape(1, half),
        shift_out.reshape(1, half),
    )
    position = lax.axis_index("block")
    live = jnp.sum(jnp.where(jnp.arange(nb, dtype=jnp.int32) == position, frame_counts, 0))
    alive = jnp.arange(SL, dtype=jnp.int32) < live
    out = jnp.where(alive[:, None, None], raw, jnp.zeros_like(raw))
    return jnp.swapaxes(out, 1, 2)[:, None]


def solution(mesh):
    return jax.shard_map(
        shards,
        mesh=mesh,
        in_specs=(
            P(("video", "block"), "band", None),
            P("video"),
            P(),
            P(),
            P(),
            P(None, None, None, None, "chan"),
            P("chan"),
            P("chan"),
        ),
        out_specs=P(("video", "block"), "band", None, "chan"),
        check_vma=False,
    )
```

time: 122 us -> 24.2 us (0.20)
  blocking collectives: 42.1 us -> 0 us
  local copies, waits for them, and re-layouts: 44.2 us -> 2.52 us
  Pallas kernels: 0 us -> 18.5 us
  other arithmetic: 16.3 us -> 2.97 us
  starting transfers between devices: 11.7 us -> 0 us
  matrix products: 6.32 us -> 0 us
    all_gather x3 -> x0, blocking collectives: 32.2 us -> none  [the longest x1 15.1 us: shards(): all_slots = lax.all_gather(latents, 'block', axis=0, tiled=True)]
    pallas_call x0 -> x1, Pallas kernels: none -> 18.5 us  [shards(): pl.pallas_call(functools.partial(body, nb, R, COLS, SL, reach), out_shape...]
    slice x22 -> x0, local copies, waits for them, and re-layouts: 17.8 us -> none  [the longest x10 8.19 us: latent_conv(): latent_grid[step_t:step_t + out_frames, step_y:step_y + band_rows, step_x...]
    ppermute x4 -> x0, starting transfers between devices: 11.7 us -> none  [the longest x2 9.11 us: with_halo(): lax.ppermute(tail, axis, [(i, (i + 1) % count) for i in range(ends)])]
    unnamed x67 -> x2, local copies, waits for them, and re-layouts: 11 us -> 0.01 us
    concatenate x12 -> x0, local copies, waits for them, and re-layouts: 9.93 us -> none  [the longest x9 5.64 us: weighted_taps(): stacked = jnp.concatenate(patches, axis=-1).reshape(-1, 3 * in_width)]
    psum x2 -> x0, blocking collectives: 9.85 us -> none  [group_silu(): lax.psum((jnp.sum(grouped, axis=(1, 3)), jnp.sum(grouped * grouped, axis=...]
    concatenate x11 -> x0, other arithmetic: 7.89 us -> none  [the longest x9 7.39 us: weighted_taps(): stacked = jnp.concatenate(patches, axis=-1).reshape(-1, 3 * in_width)]
  transfers between devices with their start and end apart: 4 -> 0, of which waited for: 0 -> 0; matrix products, arithmetic and copies ran while one was open for 17% -> 0% of each run, Pallas kernels for 0% -> 0%
where the time goes in v1:
time: 24.2 us; the launch traced here: 24 us
  Pallas kernels  18.5 us (76%)
  other arithmetic  2.97 us (12%)
  local copies, waits for them, and re-layouts  2.52 us (10%)
    pallas_call x1, Pallas kernels, shards(): pl.pallas_call(functools.partial(body, nb, R, COLS, SL, reach), out_shape...  18.5 us
    broadcast_in_dim x1, other arithmetic, shards(): return jnp.swapaxes(out, 1, 2)[:, None]  1.69 us
    reshape x1, local copies, waits for them, and re-layouts, shards(): gain_in.reshape(1, C)  1.26 us
    reshape x1, local copies, waits for them, and re-layouts, shards(): shift_in.reshape(1, C)  1.26 us
    lt x1, other arithmetic, shards(): alive = jnp.arange(SL, dtype=jnp.int32) < live  0.65 us
    reduce_sum x1, other arithmetic, shards(): jnp.sum(jnp.where(jnp.arange(nb, dtype=jnp.int32) == position, frame_coun...  0.63 us

profile of v1, /device:TPU:0, one launch (start us, length us, event | category | flops | bytes accessed | tf_op | source)
XLA Modules:
  0.0 24.0 jit_solution(6020556758127022716)
XLA Ops:
  0.0 0.0 copy-start
  0.0 1.3 %reshape.24.gin_ref = f32[1,384]{1,0:T(1,128)} reshape(f32[384]{0:T(512)} %param.11) | data formatting | bytes 3072 | tf_op jit(solution)/shard_map/reshape | solution.py:369
  1.3 1.3 %reshape.25.sin_ref = f32[1,384]{1,0:T(1,128)} reshape(f32[384]{0:T(512)} %param.12) | data formatting | bytes 3072 | tf_op jit(solution)/shard_map/reshape | solution.py:370
  2.5 18.5 %shard_map.82 = bf16[4,192,104]{2,1,0:T(8,128)(2,1)} custom-call(s32[4]{0:T(128)} %cnt_ref.1, bf16[4,1664]{1,0:T(4,128)(2,1)} %bitcast.13, bf16[3,144,384]{2,1,0:T(8,128)(2,1)} %bitcast.12, f32[1,384]{1,0:T(1,128)} %reshape.24.gin_ref, f32[1,384]{1,0:T(1,128)} %reshape.25.sin_ref, bf16[3,3,3,192,384]{4,3,2,1,0:T(8,128)(2,1)} %bitcast.11, f32[1,192]{1,0:T(1,128)} %bitcast.14, ...), custom_call_target="tpu_custom_call" | custom-call | tf_op jit(solution)/shard_map/pallas_call | solution.py:338
  21.0 0.0 copy-done
  21.0 0.6 %fusion = s32[]{:T(128)} fusion(s32[4]{0:T(128)S(1)} %copy-done, s32[]{:T(128)S(6)} %axis_index.15), kind=kLoop, calls=%fused_computation.2 | loop fusion | flops 11 | bytes 24 | tf_op jit(solution)/shard_map/reduce_sum | solution.py:376
  21.6 0.6 %iota_compare_fusion = pred[4]{0:T(512)(128)(4,1)S(1)} fusion(s32[]{:T(128)} %fusion), kind=kLoop, calls=%fused_computation.3 | loop fusion | flops 4 | bytes 8 | tf_op jit(solution)/shard_map/lt | solution.py:377
  22.3 1.7 %select_bitcast_fusion = bf16[4,1,104,192]{2,3,1,0:T(8,128)(2,1)} fusion(bf16[4,192,104]{2,1,0:T(8,128)(2,1)} %shard_map.82, pred[4]{0:T(512)(128)(4,1)S(1)} %iota_compare_fusion), kind=kLoop, calls=%fused_computation | loop fusion | flops 79872 | bytes 319492 | tf_op jit(solution)/shard_map/broadcast_in_dim | solution.py:379
Async XLA Ops:
  0.0 21.0 %copy-start = (s32[4]{0:T(128)S(1)}, s32[4]{0:T(128)}, u32[]{:S(2)}) copy-start(s32[4]{0:T(128)} %cnt_ref.1) | copy-start | bytes 52

commit v2 on v1

--- a/solution.py
+++ b/solution.py
@@ -44,16 +44,17 @@
     return y[:n] + y[n : 2 * n] + y[2 * n :]
 
 
-def silu(u):
-    return u / (1.0 + jnp.exp(-u))
+def silu_twice(v):
+    return v + v * jnp.tanh(v)
 
 
 def body(
     nb, R, COLS, SL, reach,
-    cnt_ref, lat_ref, win_ref, gin_ref, sin_ref, wmid_ref, gout_ref, sout_ref,
+    cnt_hbm, lat_ref, win_ref, gin_hbm, sin_hbm, wmid_ref, gout_hbm, sout_hbm,
     out_ref,
+    cnt_ref, gin_ref, sin_ref, gout_ref, sout_ref,
     slots, xf, gf, wpad, c1s, la, lb, wv, stats,
-    send_sem, recv_sem, st_send, st_recv, w_sem, win_sem,
+    send_sem, recv_sem, st_send, st_recv, w_sem, win_sem, in_sem,
 ):
     k = lax.axis_index("block")
     b = lax.axis_index("band")
@@ -93,12 +94,17 @@
                 device_id={"block": k - d, "band": lax.rem(b + R - o, R)},
                 device_id_type=MESH,
             )
-    for c in wincopies:
+    small = [
+        pltpu.make_async_copy(src, dst, in_sem.at[i])
+        for i, (src, dst) in enumerate(
+            [
+                (lat_ref, slots.at[0, b]), (cnt_hbm, cnt_ref), (gin_hbm, gin_ref),
+                (sin_hbm, sin_ref), (gout_hbm, gout_ref), (sout_hbm, sout_ref),
+            ]
+        )
+    ]
+    for c in small + wincopies + wcopies:
         c.start()
-    for c in wcopies:
-        c.start()
-    own = lat_ref[...]
-    slots[0, b] = own
     for r in range(R):
         size = len(rows_for(r, R)) * 3 * LAT
         if size < kpad:
@@ -140,21 +146,26 @@
         sel[rows] = jnp.where(hit, 1.0, 0.0).astype(BF16)
     gmat = group_matrix(C)
 
+    small[1].wait()
     e = [jnp.int32(0)]
     for d in range(1, reach + 1):
         n = cnt_ref[jnp.maximum(k - d, 0)]
         e.append(e[-1] + jnp.where(k >= d, n, 0))
     before = e[-1]
-
-    for d, o in pairs:
-        @pl.when(k >= d)
-        def _():
-            copy_from(d, o).wait_recv()
-
-    for d in range(reach + 1):
-        for r in range(R):
-            xf[d * R + r] = slots[d, r].astype(F32)
-
+    live = cnt_ref[k]
+
+    def arrived(some):
+        for d, o in pairs:
+            if d in some:
+                @pl.when(k >= d)
+                def _():
+                    copy_from(d, o).wait_recv()
+        for d in some:
+            for r in range(R):
+                xf[d * R + r] = slots[d, r].astype(F32)
+
+    small[0].wait()
+    arrived((0,))
     W = COLS * LAT
     lane = lax.broadcasted_iota(jnp.int32, (8, W), 1)
     sub = lax.broadcasted_iota(jnp.int32, (8, W), 0)
@@ -189,7 +200,9 @@
             for y in ys
         ]
 
-    for p in range(FL // 2):
+    for p in reversed(range(FL // 2)):
+        if p == 1:
+            arrived(range(1, reach + 1))
         ex = {}
         for r in range(R):
             u, v = expanded(2 * p, r), expanded(2 * p + 1, r)
@@ -203,12 +216,15 @@
     for c in wincopies:
         c.wait()
     MA = FA * COLS
-    for r in range(R):
-        i = sets.index(rows_for(r, R))
+    for i, rows in enumerate(sets):
+        mine = [r for r in range(R) if rows_for(r, R) == rows]
         lhs = jnp.concatenate(
             [gf[i, t * COLS : t * COLS + MA, :] for t in range(3)], axis=1
         ).astype(BF16)
-        c1s[r] = jnp.dot(lhs, wpad[r], preferred_element_type=F32).astype(BF16).astype(F32)
+        rhs = jnp.concatenate([wpad[r] for r in mine], axis=1)
+        y = jnp.dot(lhs, rhs, preferred_element_type=F32).astype(BF16).astype(F32)
+        for at, r in enumerate(mine):
+            c1s[r] = y[:, at * C : (at + 1) * C]
 
     s1, s2 = [], []
     for f in range(FA):
@@ -227,8 +243,10 @@
     mean = g[:FA] / total
     var = g[FA : 2 * FA] / total - mean * mean
     inv = lax.rsqrt(var + EPSILON)
-    scale = inv * gin_ref[...]
-    shift = sin_ref[...] - mean * scale
+    for c in small[2:]:
+        c.wait()
+    scale = inv * (0.5 * gin_ref[...].reshape(1, C))
+    shift = 0.5 * sin_ref[...].reshape(1, C) - mean * scale
 
     off = 0 if R == 2 else 1
     if off:
@@ -239,7 +257,7 @@
         act = []
         for f in range(FA):
             u = c1s[r, f * COLS : (f + 1) * COLS, :] * scale[f : f + 1] + shift[f : f + 1]
-            a = silu(u)
+            a = silu_twice(u)
             if f < 2:
                 a = jnp.where(jnp.broadcast_to(before >= 2 - f, a.shape), a, 0.0)
             act.append(a)
@@ -307,10 +325,11 @@
     mean = g[:SL] / total
     var = g[SL : 2 * SL] / total - mean * mean
     inv = lax.rsqrt(var + EPSILON)
-    scale = inv * gout_ref[...]
-    shift = sout_ref[...] - mean * scale
+    scale = inv * (0.5 * gout_ref[...].reshape(1, half))
+    shift = 0.5 * sout_ref[...].reshape(1, half) - mean * scale
     for f in range(SL):
-        a = silu(hs[f] * scale[f : f + 1] + shift[f : f + 1])
+        a = silu_twice(hs[f] * scale[f : f + 1] + shift[f : f + 1])
+        a = jnp.where(jnp.broadcast_to(f < live, a.shape), a, 0.0)
         out_ref[f] = a.T.astype(BF16)
 
     for d, o in pairs:
@@ -334,15 +353,18 @@
     kpad = up(max(len(s) for s in sets) * 3 * LAT, 128)
     extra = 0 if R == 2 else 2
     vmem = pl.BlockSpec(memory_space=pltpu.VMEM)
-    hbm = pl.BlockSpec(memory_space=pl.ANY)
+    hbm = pl.BlockSpec(memory_space=pltpu.HBM)
     raw = pl.pallas_call(
         functools.partial(body, nb, R, COLS, SL, reach),
         out_shape=jax.ShapeDtypeStruct((SL, half, COLS), BF16),
-        in_specs=[
-            pl.BlockSpec(memory_space=pltpu.SMEM), vmem, hbm, vmem, vmem, hbm, vmem, vmem,
-        ],
+        in_specs=[hbm] * 8,
         out_specs=vmem,
         scratch_shapes=[
+            pltpu.SMEM(frame_counts.shape, jnp.int32),
+            pltpu.VMEM((C,), F32),
+            pltpu.VMEM((C,), F32),
+            pltpu.VMEM((half,), F32),
+            pltpu.VMEM((half,), F32),
             pltpu.VMEM((reach + 1, R, SL, width), BF16),
             pltpu.VMEM(((reach + 1) * R, SL, width), F32),
             pltpu.VMEM((len(sets), FL * COLS, kpad), F32),
@@ -358,25 +380,22 @@
             pltpu.SemaphoreType.DMA((R,)),
             pltpu.SemaphoreType.DMA((3,)),
             pltpu.SemaphoreType.DMA((R, 3)),
+            pltpu.SemaphoreType.DMA((6,)),
         ],
         compiler_params=pltpu.CompilerParams(
-            collective_id=0, has_side_effects=True, vmem_limit_bytes=56 * 1024 * 1024
+            collective_id=0, has_side_effects=True, vmem_limit_bytes=24 * 1024 * 1024
         ),
     )(
         frame_counts,
         latents.reshape(SL, width),
         w_in.reshape(3, 9 * LAT, C),
-        gain_in.reshape(1, C),
-        shift_in.reshape(1, C),
+        gain_in,
+        shift_in,
         jnp.swapaxes(w_mid, 3, 4),
-        gain_out.reshape(1, half),
-        shift_out.reshape(1, half),
+        gain_out,
+        shift_out,
     )
-    position = lax.axis_index("block")
-    live = jnp.sum(jnp.where(jnp.arange(nb, dtype=jnp.int32) == position, frame_counts, 0))
-    alive = jnp.arange(SL, dtype=jnp.int32) < live
-    out = jnp.where(alive[:, None, None], raw, jnp.zeros_like(raw))
-    return jnp.swapaxes(out, 1, 2)[:, None]
+    return jnp.swapaxes(raw, 1, 2)[:, None]
 
 
 def solution(mesh):

time: 24.2 us -> 24.8 us (1.025)
  local copies, waits for them, and re-layouts: 2.52 us -> 7.86 us
  other arithmetic: 2.97 us -> 0 us
  Pallas kernels: 18.5 us -> 16.6 us
    unnamed x2 -> x17, local copies, waits for them, and re-layouts: 0.01 us -> 7.86 us
    reshape x2 -> x0, local copies, waits for them, and re-layouts: 2.51 us -> none  [the longest x1 1.26 us: shards(): gain_in.reshape(1, C)]
    pallas_call x1, Pallas kernels: 18.5 us -> 16.6 us  [shards(): pl.pallas_call(functools.partial(body, nb, R, COLS, SL, reach), out_shape...]
    broadcast_in_dim x1 -> x0, other arithmetic: 1.69 us -> none  [shards(): return jnp.swapaxes(out, 1, 2)[:, None]]
    lt x1 -> x0, other arithmetic: 0.65 us -> none  [shards(): alive = jnp.arange(SL, dtype=jnp.int32) < live]
    reduce_sum x1 -> x0, other arithmetic: 0.63 us -> none  [shards(): jnp.sum(jnp.where(jnp.arange(nb, dtype=jnp.int32) == position, frame_coun...]
where the time goes in v2:
time: 24.8 us; the launch traced here: 24.5 us
  Pallas kernels  16.6 us (67%)
  local copies, waits for them, and re-layouts  7.86 us (32%)
    pallas_call x1, Pallas kernels, shards(): pl.pallas_call(functools.partial(body, nb, R, COLS, SL, reach), out_shape...  16.6 us
    unnamed x17, local copies, waits for them, and re-layouts  7.86 us

profile of v2, /device:TPU:0, one launch (start us, length us, event | category | flops | bytes accessed | tf_op | source)
XLA Modules:
  0.0 24.5 jit_solution(18028641124652568080)
XLA Ops:
  0.0 0.0 copy-start
  0.0 2.1 %copy-done = bf16[3,3,3,384,192]{3,4,2,1,0:T(8,128)(2,1)S(1)} copy-done((bf16[3,3,3,384,192]{3,4,2,1,0:T(8,128)(2,1)S(1)}, bf16[3,3,3,384,192]{3,4,2,1,0:T(8,128)(2,1)}, u32[]{:S(2)}) %copy-start) | copy-done | bytes 3981336
  2.1 0.0 copy-start.1
  2.1 1.0 %copy-done.1 = bf16[3,3,3,16,384]{4,3,2,1,0:T(8,128)(2,1)S(1)} copy-done((bf16[3,3,3,16,384]{4,3,2,1,0:T(8,128)(2,1)S(1)}, bf16[3,3,3,16,384]{4,3,2,1,0:T(8,128)(2,1)}, u32[]{:S(2)}) %copy-start.1) | copy-done | bytes 331800
  3.1 0.0 copy-start.2
  3.1 0.7 %copy-done.2 = bf16[4,1,1664]{2,0,1:T(4,128)(2,1)S(1)} copy-done((bf16[4,1,1664]{2,0,1:T(4,128)(2,1)S(1)}, bf16[4,1,1664]{2,0,1:T(4,128)(2,1)}, u32[]{:S(2)}) %copy-start.2) | copy-done | bytes 13336
  3.8 0.0 copy-start.3
  3.8 0.7 %copy-done.3 = f32[384]{0:T(512)S(1)} copy-done((f32[384]{0:T(512)S(1)}, f32[384]{0:T(512)}, u32[]{:S(2)}) %copy-start.3) | copy-done | bytes 1560
  4.5 0.0 copy-start.4
  4.5 0.7 %copy-done.4 = f32[384]{0:T(512)S(1)} copy-done((f32[384]{0:T(512)S(1)}, f32[384]{0:T(512)}, u32[]{:S(2)}) %copy-start.4) | copy-done | bytes 1560
  5.2 0.0 copy-start.5
  5.2 0.7 %copy-done.5 = f32[192]{0:T(256)S(1)} copy-done((f32[192]{0:T(256)S(1)}, f32[192]{0:T(256)}, u32[]{:S(2)}) %copy-start.5) | copy-done | bytes 792
  5.9 0.0 copy-start.6
  5.9 0.7 %copy-done.6 = f32[192]{0:T(256)S(1)} copy-done((f32[192]{0:T(256)S(1)}, f32[192]{0:T(256)}, u32[]{:S(2)}) %copy-start.6) | copy-done | bytes 792
  6.5 0.0 copy-start.7
  6.5 0.7 %copy-done.7 = s32[4]{0:T(128)S(1)} copy-done((s32[4]{0:T(128)S(1)}, s32[4]{0:T(128)}, u32[]{:S(2)}) %copy-start.7) | copy-done | bytes 40
  7.2 16.6 %shard_map.82 = bf16[4,192,104]{2,1,0:T(8,128)(2,1)S(1)} custom-call(s32[4]{0:T(128)S(1)} %copy-done.7, bf16[4,1664]{1,0:T(4,128)(2,1)S(1)} %bitcast.11, bf16[3,144,384]{2,1,0:T(8,128)(2,1)S(1)} %bitcast.10, f32[384]{0:T(512)S(1)} %copy-done.3, f32[384]{0:T(512)S(1)} %copy-done.4, bf16[3,3,3,192,384]{4,3,2,1,0:T(8,128)(2,1)S(1)} %bitcast.8, ...), custom_call_target="tpu_custom_call" | custom-call | tf_op jit(solution)/shard_map/pallas_call | solution.py:357
  23.8 0.7 %copy.11 = bf16[4,1,104,192]{2,3,1,0:T(8,128)(2,1)} copy(bf16[4,1,104,192]{2,3,1,0:T(8,128)(2,1)S(1)} %bitcast.9) | data formatting | bytes 319488
Async XLA Ops:
  0.0 2.1 %copy-start = (bf16[3,3,3,384,192]{3,4,2,1,0:T(8,128)(2,1)S(1)}, bf16[3,3,3,384,192]{3,4,2,1,0:T(8,128)(2,1)}, u32[]{:S(2)}) copy-start(bf16[3,3,3,384,192]{3,4,2,1,0:T(8,128)(2,1)} %param.13) | copy-start | bytes 11943940
  2.1 1.0 %copy-start.1 = (bf16[3,3,3,16,384]{4,3,2,1,0:T(8,128)(2,1)S(1)}, bf16[3,3,3,16,384]{4,3,2,1,0:T(8,128)(2,1)}, u32[]{:S(2)}) copy-start(bf16[3,3,3,16,384]{4,3,2,1,0:T(8,128)(2,1)} %param.10) | copy-start | bytes 995332
  3.1 0.7 %copy-start.2 = (bf16[4,1,1664]{2,0,1:T(4,128)(2,1)S(1)}, bf16[4,1,1664]{2,0,1:T(4,128)(2,1)}, u32[]{:S(2)}) copy-start(bf16[4,1,1664]{2,0,1:T(4,128)(2,1)} %param.8) | copy-start | bytes 39940
  3.8 0.7 %copy-start.3 = (f32[384]{0:T(512)S(1)}, f32[384]{0:T(512)}, u32[]{:S(2)}) copy-start(f32[384]{0:T(512)} %gin_hbm.1) | copy-start | bytes 4612
  4.5 0.7 %copy-start.4 = (f32[384]{0:T(512)S(1)}, f32[384]{0:T(512)}, u32[]{:S(2)}) copy-start(f32[384]{0:T(512)} %sin_hbm.1) | copy-start | bytes 4612
  5.2 0.7 %copy-start.5 = (f32[192]{0:T(256)S(1)}, f32[192]{0:T(256)}, u32[]{:S(2)}) copy-start(f32[192]{0:T(256)} %gout_hbm.1) | copy-start | bytes 2308
  5.9 0.7 %copy-start.6 = (f32[192]{0:T(256)S(1)}, f32[192]{0:T(256)}, u32[]{:S(2)}) copy-start(f32[192]{0:T(256)} %sout_hbm.1) | copy-start | bytes 2308
  6.5 0.7 %copy-start.7 = (s32[4]{0:T(128)S(1)}, s32[4]{0:T(128)}, u32[]{:S(2)}) copy-start(s32[4]{0:T(128)} %cnt_hbm.1) | copy-start | bytes 52

commit v3 on v2

--- a/solution.py
+++ b/solution.py
@@ -356,7 +356,7 @@
     hbm = pl.BlockSpec(memory_space=pltpu.HBM)
     raw = pl.pallas_call(
         functools.partial(body, nb, R, COLS, SL, reach),
-        out_shape=jax.ShapeDtypeStruct((SL, half, COLS), BF16),
+        out_shape=pltpu.VMEM((SL, half, COLS), BF16),
         in_specs=[hbm] * 8,
         out_specs=vmem,
         scratch_shapes=[
@@ -383,9 +383,9 @@
             pltpu.SemaphoreType.DMA((6,)),
         ],
         compiler_params=pltpu.CompilerParams(
-            collective_id=0, has_side_effects=True, vmem_limit_bytes=24 * 1024 * 1024
+            collective_id=0, has_side_effects=True, vmem_limit_bytes=40 * 1024 * 1024
         ),
-    )(
+    )(*[pltpu.with_memory_space_constraint(z, pltpu.HBM) for z in (
         frame_counts,
         latents.reshape(SL, width),
         w_in.reshape(3, 9 * LAT, C),
@@ -394,7 +394,7 @@
         jnp.swapaxes(w_mid, 3, 4),
         gain_out,
         shift_out,
-    )
+    )])
     return jnp.swapaxes(raw, 1, 2)[:, None]
 
 

time: 24.8 us -> 17.8 us (0.72)
  local copies, waits for them, and re-layouts: 7.86 us -> 0.68 us
  Pallas kernels: 16.6 us -> 17 us
    unnamed x17 -> x1, local copies, waits for them, and re-layouts: 7.86 us -> 0.68 us
    pallas_call x1, Pallas kernels: 16.6 us -> 17 us  [shards(): pl.pallas_call(functools.partial(body, nb, R, COLS, SL, reach), out_shape...]
where the time goes in v3:
time: 17.8 us; the launch traced here: 17.7 us
  Pallas kernels  17 us (96%)
  local copies, waits for them, and re-layouts  0.68 us (4%)
    pallas_call x1, Pallas kernels, shards(): pl.pallas_call(functools.partial(body, nb, R, COLS, SL, reach), out_shape...  17 us
    unnamed x1, local copies, waits for them, and re-layouts  0.68 us

profile of v3, /device:TPU:0, one launch (start us, length us, event | category | flops | bytes accessed | tf_op | source)
XLA Modules:
  0.0 17.7 jit_solution(9630861991810624347)
XLA Ops:
  0.0 17.0 %shard_map.82 = bf16[4,192,104]{2,1,0:T(8,128)(2,1)S(1)} custom-call(s32[4]{0:T(128)} %cnt_hbm.1, bf16[4,1664]{1,0:T(4,128)(2,1)} %bitcast.11, bf16[3,144,384]{2,1,0:T(8,128)(2,1)} %bitcast.10, f32[384]{0:T(512)} %gin_hbm.1, f32[384]{0:T(512)} %sin_hbm.1, bf16[3,3,3,192,384]{4,3,2,1,0:T(8,128)(2,1)} %bitcast.9, f32[192]{0:T(256)} %gout_hbm.1, f32[192]{0:T(256)} %sout_hbm.1), custom_call_target="tpu_custom_call" | custom-call | tf_op jit(solution)/shard_map/pallas_call | solution.py:357
  17.0 0.7 %copy.11 = bf16[4,1,104,192]{2,3,1,0:T(8,128)(2,1)} copy(bf16[4,1,104,192]{2,3,1,0:T(8,128)(2,1)S(1)} %bitcast.8) | data formatting | bytes 319488

commit v4 on v3

--- a/solution.py
+++ b/solution.py
@@ -85,8 +85,8 @@
             )
             wincopies.append(c)
     barrier = pltpu.get_barrier_semaphore()
-    pairs = [(d, o) for d in range(reach + 1) for o in range(R) if (d, o) != (0, 0)]
-    for d, o in pairs:
+    near = [(d, o) for d in range(min(reach, 1) + 1) for o in range(R) if (d, o) != (0, 0)]
+    for d, o in near:
         @pl.when(k >= d)
         def _():
             pl.semaphore_signal(
@@ -110,21 +110,20 @@
         if size < kpad:
             for t in range(3):
                 wpad[r, t * kpad + size : (t + 1) * kpad, :] = jnp.zeros((kpad - size, C), BF16)
-    pl.semaphore_wait(barrier, jnp.minimum(reach + 1, nb - k) * R - 1)
 
     def copy_to(d, o):
         return pltpu.make_async_remote_copy(
-            src_ref=lat_ref,
+            src_ref=slots.at[max(d - 1, 0), b],
             dst_ref=slots.at[d, b],
             send_sem=send_sem.at[d, o],
             recv_sem=recv_sem.at[d, o],
-            device_id={"block": k + d, "band": lax.rem(b + o, R)},
+            device_id={"block": k + min(d, 1), "band": lax.rem(b + o, R)},
             device_id_type=MESH,
         )
 
     def copy_from(d, o):
         return pltpu.make_async_remote_copy(
-            src_ref=lat_ref,
+            src_ref=slots.at[max(d - 1, 0), b],
             dst_ref=slots.at[d, lax.rem(b + R - o, R)],
             send_sem=send_sem.at[d, o],
             recv_sem=recv_sem.at[d, o],
@@ -132,10 +131,8 @@
             device_id_type=MESH,
         )
 
-    for d, o in reversed(pairs):
-        @pl.when(k + d < nb)
-        def _():
-            copy_to(d, o).start()
+    def sends(d):
+        return (k + 1 < nb) & (k >= d - 1)
 
     sel = {}
     for rows in sets:
@@ -146,6 +143,15 @@
         sel[rows] = jnp.where(hit, 1.0, 0.0).astype(BF16)
     gmat = group_matrix(C)
 
+    small[0].wait()
+    pl.semaphore_wait(barrier, R - 1 + jnp.where(k + 1 < nb, R, 0))
+    for d, o in reversed(near):
+        if d == 0:
+            copy_to(d, o).start()
+        else:
+            @pl.when(sends(d))
+            def _():
+                copy_to(d, o).start()
     small[1].wait()
     e = [jnp.int32(0)]
     for d in range(1, reach + 1):
@@ -154,18 +160,31 @@
     before = e[-1]
     live = cnt_ref[k]
 
-    def arrived(some):
-        for d, o in pairs:
-            if d in some:
+    def unpack(d):
+        for r in range(R):
+            xf[d * R + r] = slots[d, r].astype(F32)
+
+    for o in range(1, R):
+        copy_from(0, o).wait_recv()
+    unpack(0)
+
+    def earlier():
+        for d in range(1, reach + 1):
+            @pl.when(k >= d)
+            def _():
+                copy_from(d, 0).wait_recv()
+            if d < reach:
+                @pl.when(sends(d + 1))
+                def _():
+                    for o in range(R):
+                        copy_to(d + 1, o).start()
+        for d in range(1, reach + 1):
+            for o in range(1, R):
                 @pl.when(k >= d)
                 def _():
                     copy_from(d, o).wait_recv()
-        for d in some:
-            for r in range(R):
-                xf[d * R + r] = slots[d, r].astype(F32)
-
-    small[0].wait()
-    arrived((0,))
+            unpack(d)
+
     W = COLS * LAT
     lane = lax.broadcasted_iota(jnp.int32, (8, W), 1)
     sub = lax.broadcasted_iota(jnp.int32, (8, W), 0)
@@ -202,7 +221,7 @@
 
     for p in reversed(range(FL // 2)):
         if p == 1:
-            arrived(range(1, reach + 1))
+            earlier()
         ex = {}
         for r in range(R):
             u, v = expanded(2 * p, r), expanded(2 * p + 1, r)
@@ -332,10 +351,13 @@
         a = jnp.where(jnp.broadcast_to(f < live, a.shape), a, 0.0)
         out_ref[f] = a.T.astype(BF16)
 
-    for d, o in pairs:
-        @pl.when(k + d < nb)
+    for o in range(1, R):
+        copy_to(0, o).wait_send()
+    for d in range(1, reach + 1):
+        @pl.when(sends(d))
         def _():
-            copy_to(d, o).wait_send()
+            for o in range(R):
+                copy_to(d, o).wait_send()
     for o in range(1, R):
         stat_copy(o, b).wait_send()
 

time: 17.8 us -> 18.3 us (1.028)
  the two profiles are of different devices: /device:TPU:0 before, /device:TPU:28 now
where the time goes in v4:
time: 18.3 us; the launch traced here: 18.2 us
  Pallas kernels  17.5 us (96%)
  local copies, waits for them, and re-layouts  0.68 us (4%)
    pallas_call x1, Pallas kernels, shards(): pl.pallas_call(functools.partial(body, nb, R, COLS, SL, reach), out_shape...  17.5 us
    unnamed x1, local copies, waits for them, and re-layouts  0.68 us

profile of v4, /device:TPU:28, one launch (start us, length us, event | category | flops | bytes accessed | tf_op | source)
XLA Modules:
  0.0 18.2 jit_solution(10775134969934071337)
XLA Ops:
  0.0 17.5 %shard_map.82 = bf16[4,192,104]{2,1,0:T(8,128)(2,1)S(1)} custom-call(s32[4]{0:T(128)} %cnt_hbm.1, bf16[4,1664]{1,0:T(4,128)(2,1)} %bitcast.11, bf16[3,144,384]{2,1,0:T(8,128)(2,1)} %bitcast.10, f32[384]{0:T(512)} %gin_hbm.1, f32[384]{0:T(512)} %sin_hbm.1, bf16[3,3,3,192,384]{4,3,2,1,0:T(8,128)(2,1)} %bitcast.9, f32[192]{0:T(256)} %gout_hbm.1, f32[192]{0:T(256)} %sout_hbm.1), custom_call_target="tpu_custom_call" | custom-call | tf_op jit(solution)/shard_map/pallas_call | solution.py:379
  17.5 0.7 %copy.11 = bf16[4,1,104,192]{2,3,1,0:T(8,128)(2,1)} copy(bf16[4,1,104,192]{2,3,1,0:T(8,128)(2,1)S(1)} %bitcast.8) | data formatting | bytes 319488

commit v5 on v4

v5 whole, which is shorter than its diff:
```python
import functools

import jax
import jax.numpy as jnp
from jax import lax
from jax.experimental import pallas as pl
from jax.experimental.pallas import tpu as pltpu
from jax.sharding import PartitionSpec as P

LAT = 16
C = 384
GROUPS = 32
GW = C // GROUPS
EPSILON = 1e-06
MESH = pl.DeviceIdType.MESH
F32 = jnp.float32
BF16 = jnp.bfloat16


def up(n, m):
    return (n + m - 1) // m * m


def rows_for(r, R):
    return tuple(range(max(0, r - 1), min(R - 1, r + 1) + 1))


def group_matrix(n, width):
    a = lax.broadcasted_iota(jnp.int32, (n, n), 0)
    b = lax.broadcasted_iota(jnp.int32, (n, n), 1)
    for q in range(n // width - 1, 0, -1):
        a = jnp.where(a >= q * width, a - q * width, a)
        b = jnp.where(b >= q * width, b - q * width, b)
    same = ((a * 5462) >> 16) == ((b * 5462) >> 16)
    return jnp.where(same, 1.0, 0.0).astype(BF16)


def group_sums(x, gmat):
    hi = x.astype(BF16)
    rest = x - hi.astype(F32)
    mid = rest.astype(BF16)
    lo = (rest - mid.astype(F32)).astype(BF16)
    n = x.shape[0]
    y = jnp.dot(
        jnp.concatenate([hi, mid, lo], axis=0), gmat, preferred_element_type=F32
    )
    return y[:n] + y[n : 2 * n] + y[2 * n :]


def silu_twice(v):
    return v + v * jnp.tanh(v)


def body(
    nb, R, COLS, SL, reach,
    cnt_hbm, lat_ref, win_ref, gin_hbm, sin_hbm, wmid_ref, gout_hbm, sout_hbm,
    out_ref,
    cnt_ref, gin_ref, sin_ref, gout_ref, sout_ref,
    slots, xf, gf, wpad, c1s, la, lb, wv,
    send_sem, pass_sem, recv_sem, w_sem, win_sem, in_sem,
):
    k = lax.axis_index("block")
    b = lax.axis_index("band")
    half = out_ref.shape[1]
    FL = SL + 4
    FA = SL + 2

    wcopies = []
    for t in range(3):
        c = pltpu.make_async_copy(
            wmid_ref.at[t], wv.at[t], w_sem.at[t]
        )
        wcopies.append(c)
    wincopies = []
    kpad = wpad.shape[1] // 3
    for r in range(R):
        rows = rows_for(r, R)
        first = (rows[0] - r + 1) * 3 * LAT
        size = len(rows) * 3 * LAT
        for t in range(3):
            c = pltpu.make_async_copy(
                win_ref.at[t, pl.ds(first, size)],
                wpad.at[r, pl.ds(t * kpad + rows[0] * 3 * LAT, size)],
                win_sem.at[r, t],
            )
            wincopies.append(c)
    barrier = pltpu.get_barrier_semaphore()
    odd = lax.rem(k, 2) == 1
    for d in range(reach + 1):
        from_there = k >= d if d < 2 else (k >= d) & (lax.rem(k + d, 2) == 1)
        @pl.when(from_there)
        def _():
            for o in range(1 if d == 0 else 0, R):
                pl.semaphore_signal(
                    barrier, inc=1,
                    device_id={"block": k - d, "band": lax.rem(b + R - o, R)},
                    device_id_type=MESH,
                )
    small = [
        pltpu.make_async_copy(src, dst, in_sem.at[i])
        for i, (src, dst) in enumerate(
            [
                (lat_ref, slots.at[0, b]), (cnt_hbm, cnt_ref), (gin_hbm, gin_ref),
                (sin_hbm, sin_ref), (gout_hbm, gout_ref), (sout_hbm, sout_ref),
            ]
        )
    ]
    for c in small + wincopies + wcopies:
        c.start()
    for r in range(R):
        rows = rows_for(r, R)
        lo, hi = rows[0] * 3 * LAT, (rows[-1] + 1) * 3 * LAT
        for t in range(3):
            if lo:
                wpad[r, t * kpad : t * kpad + lo, :] = jnp.zeros((lo, C), BF16)
            if hi < kpad:
                wpad[r, t * kpad + hi : (t + 1) * kpad, :] = jnp.zeros((kpad - hi, C), BF16)
    def copy_to(d, o, passed=False):
        return pltpu.make_async_remote_copy(
            src_ref=slots.at[1 if passed else 0, b],
            dst_ref=slots.at[d, b],
            send_sem=(pass_sem if passed else send_sem).at[d, o],
            recv_sem=recv_sem.at[d, o],
            device_id={"block": k + d - (1 if passed else 0), "band": lax.rem(b + o, R)},
            device_id_type=MESH,
        )

    def copy_from(d, o):
        return pltpu.make_async_remote_copy(
            src_ref=slots.at[0, b],
            dst_ref=slots.at[d, lax.rem(b + R - o, R)],
            send_sem=send_sem.at[d, o],
            recv_sem=recv_sem.at[d, o],
            device_id={"block": k, "band": lax.rem(b + o, R)},
            device_id_type=MESH,
        )

    def sends(d):
        return k + d < nb if d < 2 else (k + d < nb) & odd

    def passes(d):
        return (k + d - 1 < nb) & odd

    a = lax.broadcasted_iota(jnp.int32, (R * 3 * 128, kpad), 0)
    c = lax.broadcasted_iota(jnp.int32, (R * 3 * 128, kpad), 1)
    sel = jnp.where(((a >> 7) * LAT + (a & (LAT - 1))) == c, 1.0, 0.0).astype(BF16)
    gmat = group_matrix(C, C)
    gmat2 = group_matrix(R * half, half)

    small[0].wait()
    peers = R - 1
    for d in range(1, reach + 1):
        peers = peers + jnp.where(sends(d), R, 0)
    pl.semaphore_wait(barrier, peers)
    for d in range(reach, -1, -1):
        @pl.when(sends(d))
        def _():
            for o in range(1 if d == 0 else 0, R):
                copy_to(d, o).start()
    small[1].wait()
    e = [jnp.int32(0)]
    for d in range(1, reach + 1):
        n = cnt_ref[jnp.maximum(k - d, 0)]
        e.append(e[-1] + jnp.where(k >= d, n, 0))
    before = e[-1]
    live = cnt_ref[k]

    def unpack(d):
        for r in range(R):
            xf[d * R + r] = slots[d, r].astype(F32)

    for o in range(1, R):
        copy_from(0, o).wait_recv()
    unpack(0)

    def earlier():
        for d in range(1, reach + 1):
            @pl.when(k >= d)
            def _():
                copy_from(d, 0).wait_recv()
            if d == 1:
                for e_ in range(2, reach + 1):
                    @pl.when(passes(e_))
                    def _():
                        for o in range(R):
                            copy_to(e_, o, True).start()
        for d in range(1, reach + 1):
            @pl.when(k >= d)
            def _():
                for o in range(1, R):
                    copy_from(d, o).wait_recv()
            unpack(d)

    W = COLS * LAT
    lane = lax.broadcasted_iota(jnp.int32, (8, W), 1)
    sub = lax.broadcasted_iota(jnp.int32, (8, W), 0)
    part = (lane >> 4) & 7
    mask = [part == ((sub + 7) & 7), part == sub, part == ((sub + 1) & 7)]
    zero128 = jnp.zeros((8, 128), F32)

    def expanded(j, r):
        if j >= 4:
            row = xf[r, j - 4 : j - 3, :]
        else:
            m = 4 - j
            d = jnp.int32(1)
            base = e[1]
            for q in range(1, reach):
                more = e[q] < m
                d = jnp.where(more, q + 1, d)
                base = jnp.where(more, e[q + 1], base)
            slot = jnp.clip(base - m, 0, SL - 1)
            row = xf[d * R + r, pl.ds(slot, 1), :]
            row = jnp.where(jnp.broadcast_to(before >= m, row.shape), row, 0.0)
        bc = jnp.broadcast_to(row, (8, W))
        prev = jnp.concatenate([zero128, bc[:, : W - 128]], axis=1)
        nxt = jnp.concatenate([bc[:, 128:], zero128], axis=1)
        ys = [
            jnp.where(mask[0], jnp.where(sub == 0, prev, bc), 0.0),
            jnp.where(mask[1], bc, 0.0),
            jnp.where(mask[2], jnp.where(sub == 7, nxt, bc), 0.0),
        ]
        return [
            jnp.concatenate([y[:, q * 128 : q * 128 + 128] for q in range(W // 128)], axis=0)
            for y in ys
        ]

    for p in reversed(range(FL // 2)):
        if p == 1:
            earlier()
        ex = {}
        for r in range(R):
            u, v = expanded(2 * p, r), expanded(2 * p + 1, r)
            ex[r] = [jnp.concatenate([u[x], v[x]], axis=0).astype(BF16) for x in range(3)]
        lhs = jnp.concatenate([ex[r][x] for r in range(R) for x in range(3)], axis=1)
        gf[p * 2 * COLS : (p + 1) * 2 * COLS, :] = jnp.dot(
            lhs, sel, preferred_element_type=F32
        )

    for c in wincopies:
        c.wait()
    MA = FA * COLS
    lhs = jnp.concatenate(
        [gf[t * COLS : t * COLS + MA, :] for t in range(3)], axis=1
    ).astype(BF16)
    rhs = jnp.concatenate([wpad[r] for r in range(R)], axis=1)
    y = jnp.dot(lhs, rhs, preferred_element_type=F32).astype(BF16).astype(F32)
    for r in range(R):
        c1s[r] = y[:, r * C : (r + 1) * C]

    s1, s2 = [], []
    for f in range(FA):
        a1 = a2 = None
        for r in range(R):
            h = c1s[r, f * COLS : (f + 1) * COLS, :]
            p1 = jnp.sum(h, axis=0, keepdims=True)
            p2 = jnp.sum(h * h, axis=0, keepdims=True)
            a1 = p1 if a1 is None else a1 + p1
            a2 = p2 if a2 is None else a2 + p2
        s1.append(a1)
        s2.append(a2)
    fill = jnp.zeros((16 - 2 * FA, C), F32)
    g = group_sums(jnp.concatenate(s1 + s2 + [fill], axis=0), gmat)
    total = float(R * COLS * GW)
    mean = g[:FA] / total
    var = g[FA : 2 * FA] / total - mean * mean
    inv = lax.rsqrt(var + EPSILON)
    for c in small[2:]:
        c.wait()
    scale = inv * (0.5 * gin_ref[...].reshape(1, C))
    shift = 0.5 * sin_ref[...].reshape(1, C) - mean * scale

    for r in range(R):
        act = []
        for f in range(FA):
            u = c1s[r, f * COLS : (f + 1) * COLS, :] * scale[f : f + 1] + shift[f : f + 1]
            a = silu_twice(u)
            if f < 2:
                a = jnp.where(jnp.broadcast_to(before >= 2 - f, a.shape), a, 0.0)
            act.append(a)
        for p in range(FA // 2):
            la[r, p * 2 * COLS : (p + 1) * 2 * COLS, :] = jnp.concatenate(
                act[2 * p : 2 * p + 2], axis=0
            ).astype(BF16)
        for p in range(SL // 2):
            lb[r, p * 2 * COLS : (p + 1) * 2 * COLS, :] = jnp.concatenate(
                act[2 * p + 1 : 2 * p + 3], axis=0
            ).astype(BF16)

    for c in wcopies:
        c.wait()
    M = SL * COLS
    wide = R * half
    lhs = []
    for t in range(3):
        for q in range(R):
            lhs.append(lb[q] if t == 1 else la[q, t * COLS : t * COLS + M, :])
    lhs = jnp.concatenate(lhs, axis=1)

    def taps(t, q, r, x):
        if 0 <= q - r + 1 <= 2:
            return wv[t, q - r + 1, x]
        return jnp.zeros((half, C), BF16)

    rhs = jnp.concatenate(
        [
            jnp.concatenate([taps(t, q, r, x) for t in range(3) for q in range(R)], axis=1)
            for x in range(3)
            for r in range(R)
        ],
        axis=0,
    )
    prod = lax.dot_general(lhs, rhs, (((1,), (1,)), ((), ())), preferred_element_type=F32)
    hs, t1, t2 = [], [], []
    col = lax.broadcasted_iota(jnp.int32, (COLS, wide), 0)
    for f in range(SL):
        p0, p1, p2 = [
            prod[f * COLS : (f + 1) * COLS, x * wide : (x + 1) * wide] for x in range(3)
        ]
        h = p1 + jnp.where(col == 0, 0.0, pltpu.roll(p0, 1, 0))
        h = h + jnp.where(col == COLS - 1, 0.0, pltpu.roll(p2, COLS - 1, 0))
        h = h.astype(BF16).astype(F32)
        hs.append(h)
        t1.append(jnp.sum(h, axis=0, keepdims=True))
        t2.append(jnp.sum(h * h, axis=0, keepdims=True))
    pad = jnp.zeros((16 - 2 * SL, wide), F32)
    g = group_sums(jnp.concatenate(t1 + t2 + [pad], axis=0), gmat2)
    mean = g[:SL] / total
    var = g[SL : 2 * SL] / total - mean * mean
    inv = lax.rsqrt(var + EPSILON)
    gains = jnp.concatenate([0.5 * gout_ref[...].reshape(1, half)] * R, axis=1)
    shifts = jnp.concatenate([0.5 * sout_ref[...].reshape(1, half)] * R, axis=1)
    scale = inv * gains
    shift = shifts - mean * scale
    for r in range(R):
        lo = r * half // 128 * 128
        hi = min(up((r + 1) * half, 128), wide)

        @pl.when(b == r)
        def _():
            for f in range(SL):
                u = hs[f][:, lo:hi] * scale[f : f + 1, lo:hi] + shift[f : f + 1, lo:hi]
                a = silu_twice(u)
                a = jnp.where(jnp.broadcast_to(f < live, a.shape), a, 0.0)
                out_ref[f] = a.T[r * half - lo : (r + 1) * half - lo].astype(BF16)

    for o in range(1, R):
        copy_to(0, o).wait_send()
    for d in range(1, reach + 1):
        @pl.when(sends(d))
        def _():
            for o in range(R):
                copy_to(d, o).wait_send()
    for d in range(2, reach + 1):
        @pl.when(passes(d))
        def _():
            for o in range(R):
                copy_to(d, o, True).wait_send()


def shards(latents, frame_counts, w_in, gain_in, shift_in, w_mid, gain_out, shift_out):
    SL, band_rows, width = latents.shape
    COLS = width // LAT
    half = w_mid.shape[4]
    R = lax.axis_size("band") * band_rows
    nb = lax.axis_size("block")
    reach = min(4, nb - 1)
    FL, FA = SL + 4, SL + 2
    kpad = up(R * 3 * LAT, 128)
    vmem = pl.BlockSpec(memory_space=pltpu.VMEM)
    hbm = pl.BlockSpec(memory_space=pltpu.HBM)
    raw = pl.pallas_call(
        functools.partial(body, nb, R, COLS, SL, reach),
        out_shape=pltpu.VMEM((SL, half, COLS), BF16),
        in_specs=[hbm] * 8,
        out_specs=vmem,
        scratch_shapes=[
            pltpu.SMEM(frame_counts.shape, jnp.int32),
            pltpu.VMEM((C,), F32),
            pltpu.VMEM((C,), F32),
            pltpu.VMEM((half,), F32),
            pltpu.VMEM((half,), F32),
            pltpu.VMEM((reach + 1, R, SL, width), BF16),
            pltpu.VMEM(((reach + 1) * R, SL, width), F32),
            pltpu.VMEM((FL * COLS, kpad), F32),
            pltpu.VMEM((R, 3 * kpad, C), BF16),
            pltpu.VMEM((R, FA * COLS, C), F32),
            pltpu.VMEM((R, FA * COLS, C), BF16),
            pltpu.VMEM((R, SL * COLS, C), BF16),
            pltpu.VMEM((3, 3, 3, half, C), BF16),
            pltpu.SemaphoreType.DMA((reach + 1, R)),
            pltpu.SemaphoreType.DMA((reach + 1, R)),
            pltpu.SemaphoreType.DMA((reach + 1, R)),
            pltpu.SemaphoreType.DMA((3,)),
            pltpu.SemaphoreType.DMA((R, 3)),
            pltpu.SemaphoreType.DMA((6,)),
        ],
        compiler_params=pltpu.CompilerParams(
            collective_id=0, has_side_effects=True, vmem_limit_bytes=40 * 1024 * 1024
        ),
    )(*[pltpu.with_memory_space_constraint(z, pltpu.HBM) for z in (
        frame_counts,
        latents.reshape(SL, width),
        w_in.reshape(3, 9 * LAT, C),
        gain_in,
        shift_in,
        jnp.swapaxes(w_mid, 3, 4),
        gain_out,
        shift_out,
    )])
    return jnp.swapaxes(raw, 1, 2)[:, None]


def solution(mesh):
    return jax.shard_map(
        shards,
        mesh=mesh,
        in_specs=(
            P(("video", "block"), "band", None),
            P("video"),
            P(),
            P(),
            P(),
            P(None, None, None, None, "chan"),
            P("chan"),
            P("chan"),
        ),
        out_specs=P(("video", "block"), "band", None, "chan"),
        check_vma=False,
    )
```

time: 18.3 us -> 16.2 us (0.89)
  Pallas kernels: 17.5 us -> 15.4 us
    pallas_call x1, Pallas kernels: 17.5 us -> 15.4 us  [shards(): pl.pallas_call(functools.partial(body, nb, R, COLS, SL, reach), out_shape...]
where the time goes in v5:
time: 16.2 us; the launch traced here: 16.1 us
  Pallas kernels  15.4 us (95%)
  local copies, waits for them, and re-layouts  0.68 us (4%)
    pallas_call x1, Pallas kernels, shards(): pl.pallas_call(functools.partial(body, nb, R, COLS, SL, reach), out_shape...  15.4 us
    unnamed x1, local copies, waits for them, and re-layouts  0.68 us

profile of v5, /device:TPU:28, one launch (start us, length us, event | category | flops | bytes accessed | tf_op | source)
XLA Modules:
  0.0 16.1 jit_solution(15353897313656036028)
XLA Ops:
  0.0 15.4 %shard_map.82 = bf16[4,192,104]{2,1,0:T(8,128)(2,1)S(1)} custom-call(s32[4]{0:T(128)} %cnt_hbm.1, bf16[4,1664]{1,0:T(4,128)(2,1)} %bitcast.11, bf16[3,144,384]{2,1,0:T(8,128)(2,1)} %bitcast.10, f32[384]{0:T(512)} %gin_hbm.1, f32[384]{0:T(512)} %sin_hbm.1, bf16[3,3,3,192,384]{4,3,2,1,0:T(8,128)(2,1)} %bitcast.9, f32[192]{0:T(256)} %gout_hbm.1, f32[192]{0:T(256)} %sout_hbm.1), custom_call_target="tpu_custom_call" | custom-call | tf_op jit(solution)/shard_map/pallas_call | solution.py:372
  15.4 0.7 %copy.11 = bf16[4,1,104,192]{2,3,1,0:T(8,128)(2,1)} copy(bf16[4,1,104,192]{2,3,1,0:T(8,128)(2,1)S(1)} %bitcast.8) | data formatting | bytes 319488

commit v6 on v5

--- a/solution.py
+++ b/solution.py
@@ -157,6 +157,16 @@
         def _():
             for o in range(1 if d == 0 else 0, R):
                 copy_to(d, o).start()
+
+    @pl.when(odd)
+    def _():
+        copy_from(1, 0).wait_recv()
+        for d in range(reach, 1, -1):
+            @pl.when(passes(d))
+            def _():
+                for o in range(R):
+                    copy_to(d, o, True).start()
+
     small[1].wait()
     e = [jnp.int32(0)]
     for d in range(1, reach + 1):
@@ -175,15 +185,9 @@
 
     def earlier():
         for d in range(1, reach + 1):
-            @pl.when(k >= d)
+            @pl.when((k >= d) & ~odd if d == 1 else k >= d)
             def _():
                 copy_from(d, 0).wait_recv()
-            if d == 1:
-                for e_ in range(2, reach + 1):
-                    @pl.when(passes(e_))
-                    def _():
-                        for o in range(R):
-                            copy_to(e_, o, True).start()
         for d in range(1, reach + 1):
             @pl.when(k >= d)
             def _():

time: 16.2 us -> 14 us (0.86)
  the two profiles are of different devices: /device:TPU:28 before, /device:TPU:20 now
where the time goes in v6:
time: 14 us; the launch traced here: 13.9 us
  Pallas kernels  13.2 us (94%)
  local copies, waits for them, and re-layouts  0.68 us (5%)
    pallas_call x1, Pallas kernels, shards(): pl.pallas_call(functools.partial(body, nb, R, COLS, SL, reach), out_shape...  13.2 us
    unnamed x1, local copies, waits for them, and re-layouts  0.68 us

profile of v6, /device:TPU:20, one launch (start us, length us, event | category | flops | bytes accessed | tf_op | source)
XLA Modules:
  0.0 13.9 jit_solution(124778029167883525)
XLA Ops:
  0.0 13.2 %shard_map.82 = bf16[4,192,104]{2,1,0:T(8,128)(2,1)S(1)} custom-call(s32[4]{0:T(128)} %cnt_hbm.1, bf16[4,1664]{1,0:T(4,128)(2,1)} %bitcast.11, bf16[3,144,384]{2,1,0:T(8,128)(2,1)} %bitcast.10, f32[384]{0:T(512)} %gin_hbm.1, f32[384]{0:T(512)} %sin_hbm.1, bf16[3,3,3,192,384]{4,3,2,1,0:T(8,128)(2,1)} %bitcast.9, f32[192]{0:T(256)} %gout_hbm.1, f32[192]{0:T(256)} %sout_hbm.1), custom_call_target="tpu_custom_call" | custom-call | tf_op jit(solution)/shard_map/pallas_call | solution.py:376
  13.2 0.7 %copy.11 = bf16[4,1,104,192]{2,3,1,0:T(8,128)(2,1)} copy(bf16[4,1,104,192]{2,3,1,0:T(8,128)(2,1)S(1)} %bitcast.8) | data formatting | bytes 319488

commit v7 on v6

--- a/solution.py
+++ b/solution.py
@@ -61,6 +61,8 @@
 ):
     k = lax.axis_index("block")
     b = lax.axis_index("band")
+    cores = lax.axis_size("chan")
+    speaks = lax.axis_index("chan") == cores - 1
     half = out_ref.shape[1]
     FL = SL + 4
     FA = SL + 2
@@ -93,7 +95,7 @@
             for o in range(1 if d == 0 else 0, R):
                 pl.semaphore_signal(
                     barrier, inc=1,
-                    device_id={"block": k - d, "band": lax.rem(b + R - o, R)},
+                    device_id={"block": k - d, "band": lax.rem(b + R - o, R), "chan": cores - 1},
                     device_id_type=MESH,
                 )
     small = [
@@ -115,13 +117,17 @@
                 wpad[r, t * kpad : t * kpad + lo, :] = jnp.zeros((lo, C), BF16)
             if hi < kpad:
                 wpad[r, t * kpad + hi : (t + 1) * kpad, :] = jnp.zeros((kpad - hi, C), BF16)
-    def copy_to(d, o, passed=False):
+    def copy_to(d, o, c, passed=False):
         return pltpu.make_async_remote_copy(
             src_ref=slots.at[1 if passed else 0, b],
             dst_ref=slots.at[d, b],
-            send_sem=(pass_sem if passed else send_sem).at[d, o],
+            send_sem=(pass_sem if passed else send_sem).at[d, o, c],
             recv_sem=recv_sem.at[d, o],
-            device_id={"block": k + d - (1 if passed else 0), "band": lax.rem(b + o, R)},
+            device_id={
+                "block": k + d - (1 if passed else 0),
+                "band": lax.rem(b + o, R),
+                "chan": c,
+            },
             device_id_type=MESH,
         )
 
@@ -129,17 +135,17 @@
         return pltpu.make_async_remote_copy(
             src_ref=slots.at[0, b],
             dst_ref=slots.at[d, lax.rem(b + R - o, R)],
-            send_sem=send_sem.at[d, o],
+            send_sem=send_sem.at[d, o, 0],
             recv_sem=recv_sem.at[d, o],
             device_id={"block": k, "band": lax.rem(b + o, R)},
             device_id_type=MESH,
         )
 
     def sends(d):
-        return k + d < nb if d < 2 else (k + d < nb) & odd
+        return speaks & (k + d < nb if d < 2 else (k + d < nb) & odd)
 
     def passes(d):
-        return (k + d - 1 < nb) & odd
+        return speaks & (k + d - 1 < nb) & odd
 
     a = lax.broadcasted_iota(jnp.int32, (R * 3 * 128, kpad), 0)
     c = lax.broadcasted_iota(jnp.int32, (R * 3 * 128, kpad), 1)
@@ -148,24 +154,29 @@
     gmat2 = group_matrix(R * half, half)
 
     small[0].wait()
-    peers = R - 1
+    peers = jnp.int32(R - 1)
     for d in range(1, reach + 1):
         peers = peers + jnp.where(sends(d), R, 0)
-    pl.semaphore_wait(barrier, peers)
+    @pl.when(speaks)
+    def _():
+        pl.semaphore_wait(barrier, peers * cores)
+
     for d in range(reach, -1, -1):
         @pl.when(sends(d))
         def _():
             for o in range(1 if d == 0 else 0, R):
-                copy_to(d, o).start()
-
-    @pl.when(odd)
+                for c in range(cores):
+                    copy_to(d, o, c).start()
+
+    @pl.when(odd & speaks)
     def _():
         copy_from(1, 0).wait_recv()
         for d in range(reach, 1, -1):
             @pl.when(passes(d))
             def _():
                 for o in range(R):
-                    copy_to(d, o, True).start()
+                    for c in range(cores):
+                        copy_to(d, o, c, True).start()
 
     small[1].wait()
     e = [jnp.int32(0)]
@@ -185,7 +196,7 @@
 
     def earlier():
         for d in range(1, reach + 1):
-            @pl.when((k >= d) & ~odd if d == 1 else k >= d)
+            @pl.when((k >= d) & ~(odd & speaks) if d == 1 else k >= d)
             def _():
                 copy_from(d, 0).wait_recv()
         for d in range(1, reach + 1):
@@ -348,18 +359,18 @@
                 a = jnp.where(jnp.broadcast_to(f < live, a.shape), a, 0.0)
                 out_ref[f] = a.T[r * half - lo : (r + 1) * half - lo].astype(BF16)
 
-    for o in range(1, R):
-        copy_to(0, o).wait_send()
-    for d in range(1, reach + 1):
+    for d in range(reach + 1):
         @pl.when(sends(d))
         def _():
-            for o in range(R):
-                copy_to(d, o).wait_send()
+            for o in range(1 if d == 0 else 0, R):
+                for c in range(cores):
+                    copy_to(d, o, c).wait_send()
     for d in range(2, reach + 1):
         @pl.when(passes(d))
         def _():
             for o in range(R):
-                copy_to(d, o, True).wait_send()
+                for c in range(cores):
+                    copy_to(d, o, c, True).wait_send()
 
 
 def shards(latents, frame_counts, w_in, gain_in, shift_in, w_mid, gain_out, shift_out):
@@ -368,6 +379,7 @@
     half = w_mid.shape[4]
     R = lax.axis_size("band") * band_rows
     nb = lax.axis_size("block")
+    cores = lax.axis_size("chan")
     reach = min(4, nb - 1)
     FL, FA = SL + 4, SL + 2
     kpad = up(R * 3 * LAT, 128)
@@ -392,8 +404,8 @@
             pltpu.VMEM((R, FA * COLS, C), BF16),
             pltpu.VMEM((R, SL * COLS, C), BF16),
             pltpu.VMEM((3, 3, 3, half, C), BF16),
-            pltpu.SemaphoreType.DMA((reach + 1, R)),
-            pltpu.SemaphoreType.DMA((reach + 1, R)),
+            pltpu.SemaphoreType.DMA((reach + 1, R, cores)),
+            pltpu.SemaphoreType.DMA((reach + 1, R, cores)),
             pltpu.SemaphoreType.DMA((reach + 1, R)),
             pltpu.SemaphoreType.DMA((3,)),
             pltpu.SemaphoreType.DMA((R, 3)),

time: 14 us -> 14.3 us (1.021)
  the two profiles are of different devices: /device:TPU:20 before, /device:TPU:17 now
where the time goes in v7:
time: 14.3 us; the launch traced here: 14.2 us
  Pallas kernels  13.5 us (94%)
  local copies, waits for them, and re-layouts  0.68 us (5%)
    pallas_call x1, Pallas kernels, shards(): pl.pallas_call(functools.partial(body, nb, R, COLS, SL, reach), out_shape...  13.5 us
    unnamed x1, local copies, waits for them, and re-layouts  0.68 us

profile of v7, /device:TPU:17, one launch (start us, length us, event | category | flops | bytes accessed | tf_op | source)
XLA Modules:
  0.0 14.2 jit_solution(8578372586476143573)
XLA Ops:
  0.0 13.5 %shard_map.82 = bf16[4,192,104]{2,1,0:T(8,128)(2,1)S(1)} custom-call(s32[4]{0:T(128)} %cnt_hbm.1, bf16[4,1664]{1,0:T(4,128)(2,1)} %bitcast.11, bf16[3,144,384]{2,1,0:T(8,128)(2,1)} %bitcast.10, f32[384]{0:T(512)} %gin_hbm.1, f32[384]{0:T(512)} %sin_hbm.1, bf16[3,3,3,192,384]{4,3,2,1,0:T(8,128)(2,1)} %bitcast.9, f32[192]{0:T(256)} %gout_hbm.1, f32[192]{0:T(256)} %sout_hbm.1), custom_call_target="tpu_custom_call" | custom-call | tf_op jit(solution)/shard_map/pallas_call | solution.py:388
  13.5 0.7 %copy.11 = bf16[4,1,104,192]{2,3,1,0:T(8,128)(2,1)} copy(bf16[4,1,104,192]{2,3,1,0:T(8,128)(2,1)S(1)} %bitcast.8) | data formatting | bytes 319488

commit v8 on v6

--- a/solution.py
+++ b/solution.py
@@ -61,6 +61,9 @@
 ):
     k = lax.axis_index("block")
     b = lax.axis_index("band")
+    cores = lax.axis_size("chan")
+    core = lax.axis_index("chan")
+    passer = (lax.rem(k, 2) == 1) & (core == cores - 1)
     half = out_ref.shape[1]
     FL = SL + 4
     FA = SL + 2
@@ -96,6 +99,15 @@
                     device_id={"block": k - d, "band": lax.rem(b + R - o, R)},
                     device_id_type=MESH,
                 )
+    for d in range(1, reach):
+        @pl.when((k >= d) & (lax.rem(k + d, 2) == 1) & (core < cores - 1))
+        def _():
+            for o in range(R):
+                pl.semaphore_signal(
+                    barrier, inc=1,
+                    device_id={"block": k - d, "band": lax.rem(b + R - o, R), "chan": cores - 1},
+                    device_id_type=MESH,
+                )
     small = [
         pltpu.make_async_copy(src, dst, in_sem.at[i])
         for i, (src, dst) in enumerate(
@@ -115,13 +127,23 @@
                 wpad[r, t * kpad : t * kpad + lo, :] = jnp.zeros((lo, C), BF16)
             if hi < kpad:
                 wpad[r, t * kpad + hi : (t + 1) * kpad, :] = jnp.zeros((kpad - hi, C), BF16)
-    def copy_to(d, o, passed=False):
+    def copy_to(d, o):
         return pltpu.make_async_remote_copy(
-            src_ref=slots.at[1 if passed else 0, b],
+            src_ref=slots.at[0, b],
             dst_ref=slots.at[d, b],
-            send_sem=(pass_sem if passed else send_sem).at[d, o],
+            send_sem=send_sem.at[d, o],
             recv_sem=recv_sem.at[d, o],
-            device_id={"block": k + d - (1 if passed else 0), "band": lax.rem(b + o, R)},
+            device_id={"block": k + d, "band": lax.rem(b + o, R)},
+            device_id_type=MESH,
+        )
+
+    def pass_to(d, o, c):
+        return pltpu.make_async_remote_copy(
+            src_ref=slots.at[1, b],
+            dst_ref=slots.at[d, b],
+            send_sem=pass_sem.at[d, o, c],
+            recv_sem=recv_sem.at[d, o],
+            device_id={"block": k + d - 1, "band": lax.rem(b + o, R), "chan": c},
             device_id_type=MESH,
         )
 
@@ -139,7 +161,7 @@
         return k + d < nb if d < 2 else (k + d < nb) & odd
 
     def passes(d):
-        return (k + d - 1 < nb) & odd
+        return (k + d - 1 < nb) & passer
 
     a = lax.broadcasted_iota(jnp.int32, (R * 3 * 128, kpad), 0)
     c = lax.broadcasted_iota(jnp.int32, (R * 3 * 128, kpad), 1)
@@ -151,6 +173,8 @@
     peers = R - 1
     for d in range(1, reach + 1):
         peers = peers + jnp.where(sends(d), R, 0)
+    for d in range(2, reach + 1):
+        peers = peers + jnp.where(passes(d), R * (cores - 1), 0)
     pl.semaphore_wait(barrier, peers)
     for d in range(reach, -1, -1):
         @pl.when(sends(d))
@@ -158,14 +182,15 @@
             for o in range(1 if d == 0 else 0, R):
                 copy_to(d, o).start()
 
-    @pl.when(odd)
+    @pl.when(passer)
     def _():
         copy_from(1, 0).wait_recv()
         for d in range(reach, 1, -1):
             @pl.when(passes(d))
             def _():
-                for o in range(R):
-                    copy_to(d, o, True).start()
+                for c in range(cores):
+                    for o in range(R):
+                        pass_to(d, o, c).start()
 
     small[1].wait()
     e = [jnp.int32(0)]
@@ -185,7 +210,7 @@
 
     def earlier():
         for d in range(1, reach + 1):
-            @pl.when((k >= d) & ~odd if d == 1 else k >= d)
+            @pl.when((k >= d) & ~passer if d == 1 else k >= d)
             def _():
                 copy_from(d, 0).wait_recv()
         for d in range(1, reach + 1):
@@ -358,8 +383,9 @@
     for d in range(2, reach + 1):
         @pl.when(passes(d))
         def _():
-            for o in range(R):
-                copy_to(d, o, True).wait_send()
+            for c in range(cores):
+                for o in range(R):
+                    pass_to(d, o, c).wait_send()
 
 
 def shards(latents, frame_counts, w_in, gain_in, shift_in, w_mid, gain_out, shift_out):
@@ -368,6 +394,7 @@
     half = w_mid.shape[4]
     R = lax.axis_size("band") * band_rows
     nb = lax.axis_size("block")
+    cores = lax.axis_size("chan")
     reach = min(4, nb - 1)
     FL, FA = SL + 4, SL + 2
     kpad = up(R * 3 * LAT, 128)
@@ -393,7 +420,7 @@
             pltpu.VMEM((R, SL * COLS, C), BF16),
             pltpu.VMEM((3, 3, 3, half, C), BF16),
             pltpu.SemaphoreType.DMA((reach + 1, R)),
-            pltpu.SemaphoreType.DMA((reach + 1, R)),
+            pltpu.SemaphoreType.DMA((reach + 1, R, cores)),
             pltpu.SemaphoreType.DMA((reach + 1, R)),
             pltpu.SemaphoreType.DMA((3,)),
             pltpu.SemaphoreType.DMA((R, 3)),

time: 14 us -> 14.1 us (level)
  the two profiles are of different devices: /device:TPU:20 before, /device:TPU:17 now
where the time goes in v8:
time: 14.1 us; the launch traced here: 14 us
  Pallas kernels  13.3 us (94%)
  local copies, waits for them, and re-layouts  0.68 us (5%)
    pallas_call x1, Pallas kernels, shards(): pl.pallas_call(functools.partial(body, nb, R, COLS, SL, reach), out_shape...  13.3 us
    unnamed x1, local copies, waits for them, and re-layouts  0.68 us

profile of v8, /device:TPU:17, one launch (start us, length us, event | category | flops | bytes accessed | tf_op | source)
XLA Modules:
  0.0 14.0 jit_solution(7714610713788061163)
XLA Ops:
  0.0 13.3 %shard_map.82 = bf16[4,192,104]{2,1,0:T(8,128)(2,1)S(1)} custom-call(s32[4]{0:T(128)} %cnt_hbm.1, bf16[4,1664]{1,0:T(4,128)(2,1)} %bitcast.11, bf16[3,144,384]{2,1,0:T(8,128)(2,1)} %bitcast.10, f32[384]{0:T(512)} %gin_hbm.1, f32[384]{0:T(512)} %sin_hbm.1, bf16[3,3,3,192,384]{4,3,2,1,0:T(8,128)(2,1)} %bitcast.9, f32[192]{0:T(256)} %gout_hbm.1, f32[192]{0:T(256)} %sout_hbm.1), custom_call_target="tpu_custom_call" | custom-call | tf_op jit(solution)/shard_map/pallas_call | solution.py:403
  13.3 0.7 %copy.11 = bf16[4,1,104,192]{2,3,1,0:T(8,128)(2,1)} copy(bf16[4,1,104,192]{2,3,1,0:T(8,128)(2,1)S(1)} %bitcast.8) | data formatting | bytes 319488

commit v9 on v6

--- a/solution.py
+++ b/solution.py
@@ -161,7 +161,7 @@
     @pl.when(odd)
     def _():
         copy_from(1, 0).wait_recv()
-        for d in range(reach, 1, -1):
+        for d in range(2, reach + 1):
             @pl.when(passes(d))
             def _():
                 for o in range(R):
@@ -229,67 +229,73 @@
             for y in ys
         ]
 
-    for p in reversed(range(FL // 2)):
-        if p == 1:
-            earlier()
-        ex = {}
+    def expand_pairs(pairs):
+        for p in pairs:
+            ex = {}
+            for r in range(R):
+                u, v = expanded(2 * p, r), expanded(2 * p + 1, r)
+                ex[r] = [jnp.concatenate([u[x], v[x]], axis=0).astype(BF16) for x in range(3)]
+            lhs = jnp.concatenate([ex[r][x] for r in range(R) for x in range(3)], axis=1)
+            gf[p * 2 * COLS : (p + 1) * 2 * COLS, :] = jnp.dot(
+                lhs, sel, preferred_element_type=F32
+            )
+
+    total = float(R * COLS * GW)
+    act = {}
+
+    def first_stage(lo, hi):
+        n = hi - lo
+        lhs = jnp.concatenate(
+            [gf[(lo + t) * COLS : (hi + t) * COLS, :] for t in range(3)], axis=1
+        ).astype(BF16)
+        rhs = jnp.concatenate([wpad[r] for r in range(R)], axis=1)
+        y = jnp.dot(lhs, rhs, preferred_element_type=F32).astype(BF16).astype(F32)
         for r in range(R):
-            u, v = expanded(2 * p, r), expanded(2 * p + 1, r)
-            ex[r] = [jnp.concatenate([u[x], v[x]], axis=0).astype(BF16) for x in range(3)]
-        lhs = jnp.concatenate([ex[r][x] for r in range(R) for x in range(3)], axis=1)
-        gf[p * 2 * COLS : (p + 1) * 2 * COLS, :] = jnp.dot(
-            lhs, sel, preferred_element_type=F32
-        )
-
-    for c in wincopies:
+            c1s[r, lo * COLS : hi * COLS, :] = y[:, r * C : (r + 1) * C]
+        s1, s2 = [], []
+        for f in range(lo, hi):
+            a1 = a2 = None
+            for r in range(R):
+                h = c1s[r, f * COLS : (f + 1) * COLS, :]
+                p1 = jnp.sum(h, axis=0, keepdims=True)
+                p2 = jnp.sum(h * h, axis=0, keepdims=True)
+                a1 = p1 if a1 is None else a1 + p1
+                a2 = p2 if a2 is None else a2 + p2
+            s1.append(a1)
+            s2.append(a2)
+        fill = [jnp.zeros((16 - 2 * n, C), F32)] if n < 8 else []
+        g = group_sums(jnp.concatenate(s1 + s2 + fill, axis=0), gmat)
+        mean = g[:n] / total
+        var = g[n : 2 * n] / total - mean * mean
+        inv = lax.rsqrt(var + EPSILON)
+        scale = inv * (0.5 * gin_ref[...].reshape(1, C))
+        shift = 0.5 * sin_ref[...].reshape(1, C) - mean * scale
+        for r in range(R):
+            for f in range(lo, hi):
+                q = f - lo
+                u = c1s[r, f * COLS : (f + 1) * COLS, :] * scale[q : q + 1] + shift[q : q + 1]
+                a = silu_twice(u)
+                if f < 2:
+                    a = jnp.where(jnp.broadcast_to(before >= 2 - f, a.shape), a, 0.0)
+                act[r, f] = a
+
+    def store_pair(ref, at, r, f):
+        ref[r, at * 2 * COLS : (at + 1) * 2 * COLS, :] = jnp.concatenate(
+            [act[r, f], act[r, f + 1]], axis=0
+        ).astype(BF16)
+
+    expand_pairs(reversed(range(2, FL // 2)))
+    for c in wincopies + small[2:]:
         c.wait()
-    MA = FA * COLS
-    lhs = jnp.concatenate(
-        [gf[t * COLS : t * COLS + MA, :] for t in range(3)], axis=1
-    ).astype(BF16)
-    rhs = jnp.concatenate([wpad[r] for r in range(R)], axis=1)
-    y = jnp.dot(lhs, rhs, preferred_element_type=F32).astype(BF16).astype(F32)
+    first_stage(4, FA)
+    earlier()
+    expand_pairs((1, 0))
+    first_stage(0, 4)
     for r in range(R):
-        c1s[r] = y[:, r * C : (r + 1) * C]
-
-    s1, s2 = [], []
-    for f in range(FA):
-        a1 = a2 = None
-        for r in range(R):
-            h = c1s[r, f * COLS : (f + 1) * COLS, :]
-            p1 = jnp.sum(h, axis=0, keepdims=True)
-            p2 = jnp.sum(h * h, axis=0, keepdims=True)
-            a1 = p1 if a1 is None else a1 + p1
-            a2 = p2 if a2 is None else a2 + p2
-        s1.append(a1)
-        s2.append(a2)
-    fill = jnp.zeros((16 - 2 * FA, C), F32)
-    g = group_sums(jnp.concatenate(s1 + s2 + [fill], axis=0), gmat)
-    total = float(R * COLS * GW)
-    mean = g[:FA] / total
-    var = g[FA : 2 * FA] / total - mean * mean
-    inv = lax.rsqrt(var + EPSILON)
-    for c in small[2:]:
-        c.wait()
-    scale = inv * (0.5 * gin_ref[...].reshape(1, C))
-    shift = 0.5 * sin_ref[...].reshape(1, C) - mean * scale
-
-    for r in range(R):
-        act = []
-        for f in range(FA):
-            u = c1s[r, f * COLS : (f + 1) * COLS, :] * scale[f : f + 1] + shift[f : f + 1]
-            a = silu_twice(u)
-            if f < 2:
-                a = jnp.where(jnp.broadcast_to(before >= 2 - f, a.shape), a, 0.0)
-            act.append(a)
         for p in range(FA // 2):
-            la[r, p * 2 * COLS : (p + 1) * 2 * COLS, :] = jnp.concatenate(
-                act[2 * p : 2 * p + 2], axis=0
-            ).astype(BF16)
+            store_pair(la, p, r, 2 * p)
         for p in range(SL // 2):
-            lb[r, p * 2 * COLS : (p + 1) * 2 * COLS, :] = jnp.concatenate(
-                act[2 * p + 1 : 2 * p + 3], axis=0
-            ).astype(BF16)
+            store_pair(lb, p, r, 2 * p + 1)
 
     for c in wcopies:
         c.wait()

time: 14 us -> 13.4 us (0.957)
  the two profiles are of different devices: /device:TPU:20 before, /device:TPU:0 now
where the time goes in v9:
time: 13.4 us; the launch traced here: 13.2 us
  Pallas kernels  12.5 us (93%)
  local copies, waits for them, and re-layouts  0.68 us (5%)
    pallas_call x1, Pallas kernels, shards(): pl.pallas_call(functools.partial(body, nb, R, COLS, SL, reach), out_shape...  12.5 us
    unnamed x1, local copies, waits for them, and re-layouts  0.68 us

profile of v9, /device:TPU:0, one launch (start us, length us, event | category | flops | bytes accessed | tf_op | source)
XLA Modules:
  0.0 13.2 jit_solution(16994276090224365588)
XLA Ops:
  0.0 12.5 %shard_map.82 = bf16[4,192,104]{2,1,0:T(8,128)(2,1)S(1)} custom-call(s32[4]{0:T(128)} %cnt_hbm.1, bf16[4,1664]{1,0:T(4,128)(2,1)} %bitcast.11, bf16[3,144,384]{2,1,0:T(8,128)(2,1)} %bitcast.10, f32[384]{0:T(512)} %gin_hbm.1, f32[384]{0:T(512)} %sin_hbm.1, bf16[3,3,3,192,384]{4,3,2,1,0:T(8,128)(2,1)} %bitcast.9, f32[192]{0:T(256)} %gout_hbm.1, f32[192]{0:T(256)} %sout_hbm.1), custom_call_target="tpu_custom_call" | custom-call | tf_op jit(solution)/shard_map/pallas_call | solution.py:382
  12.5 0.7 %copy.11 = bf16[4,1,104,192]{2,3,1,0:T(8,128)(2,1)} copy(bf16[4,1,104,192]{2,3,1,0:T(8,128)(2,1)S(1)} %bitcast.8) | data formatting | bytes 319488

commit v10 on v9

--- a/solution.py
+++ b/solution.py
@@ -152,7 +152,7 @@
     for d in range(1, reach + 1):
         peers = peers + jnp.where(sends(d), R, 0)
     pl.semaphore_wait(barrier, peers)
-    for d in range(reach, -1, -1):
+    for d in range(reach + 1):
         @pl.when(sends(d))
         def _():
             for o in range(1 if d == 0 else 0, R):

time: 13.4 us -> 13.4 us (level)
  no operation moved by 1% of the time
where the time goes in v10:
time: 13.4 us; the launch traced here: 13.2 us
  Pallas kernels  12.5 us (93%)
  local copies, waits for them, and re-layouts  0.68 us (5%)
    pallas_call x1, Pallas kernels, shards(): pl.pallas_call(functools.partial(body, nb, R, COLS, SL, reach), out_shape...  12.5 us
    unnamed x1, local copies, waits for them, and re-layouts  0.68 us

profile of v10, /device:TPU:0, one launch (start us, length us, event | category | flops | bytes accessed | tf_op | source)
XLA Modules:
  0.0 13.2 jit_solution(15575876690295882820)
XLA Ops:
  0.0 12.5 %shard_map.82 = bf16[4,192,104]{2,1,0:T(8,128)(2,1)S(1)} custom-call(s32[4]{0:T(128)} %cnt_hbm.1, bf16[4,1664]{1,0:T(4,128)(2,1)} %bitcast.11, bf16[3,144,384]{2,1,0:T(8,128)(2,1)} %bitcast.10, f32[384]{0:T(512)} %gin_hbm.1, f32[384]{0:T(512)} %sin_hbm.1, bf16[3,3,3,192,384]{4,3,2,1,0:T(8,128)(2,1)} %bitcast.9, f32[192]{0:T(256)} %gout_hbm.1, f32[192]{0:T(256)} %sout_hbm.1), custom_call_target="tpu_custom_call" | custom-call | tf_op jit(solution)/shard_map/pallas_call | solution.py:382
  12.5 0.7 %copy.11 = bf16[4,1,104,192]{2,3,1,0:T(8,128)(2,1)} copy(bf16[4,1,104,192]{2,3,1,0:T(8,128)(2,1)S(1)} %bitcast.8) | data formatting | bytes 319488
